TPU v7x, 512 devices: a whole 4x4x16 slice. The times are simulated.
512 devices in a mesh: rep: 8 (over z_lo), fsdp: 16 (over z_hi, y, core), tp: 4 (over x).
Axes of the slice: x: 4, y: 4, z: 16 (z_hi: 2, z_lo: 8; z = z_hi * 8 + z_lo), core: 2. Of those that a mesh axis runs over, the one named last changes fastest.
Arguments:
- local_params: bfloat16 [8, 256, 32768], P('rep', 'fsdp', 'tp'), may hold values from -6 to 6
- global_owned: float32 [16, 16, 32768], P('rep', 'fsdp', 'tp'), may hold values from -6 to 6
- momentum: float32 [16, 16, 32768], P('rep', 'fsdp', 'tp'), may hold values from -4 to 4
Outputs:
- global_next: float32 [16, 16, 32768], P('rep', 'fsdp', 'tp')
- momentum_next: float32 [16, 16, 32768], P('rep', 'fsdp', 'tp')
- replica_params: bfloat16 [256, 32768], P('fsdp', 'tp')
All inputs are finite; a program needn't handle non-finite values.
Results may differ from a plain program's by a relative error of at most 0.015.
Values may be sent and summed in bfloat16 or wider, within the bound.
No kernel may reach another device: no remote copies, remote signals or barrier semaphores. Data moves between devices by JAX's collectives and lax.ppermute only.
A program may use at most 192 MiB of HBM per device.

v0:
```python
import jax
import jax.numpy as jnp
from jax import lax
from jax.sharding import PartitionSpec as P


def outer_update(summed, replicas, global_owned, momentum):
    mean_local = summed / replicas
    pseudo_grad = global_owned - mean_local
    moment_new = 0.9 * momentum + pseudo_grad
    global_new = global_owned - 0.7 * (pseudo_grad + 0.9 * moment_new)
    return (global_new, moment_new)


def body(local_params, global_owned, momentum):
    groups = lax.axis_size("fsdp")
    replicas = lax.axis_size("rep")
    rows_here = local_params.shape[1]
    width = local_params.shape[2]
    piece_rows = rows_here // groups
    blocks = local_params[0].reshape(groups, piece_rows, width)
    relaid = lax.all_to_all(blocks, "fsdp", split_axis=0, concat_axis=0, tiled=True)
    summed = lax.psum_scatter(
        relaid.astype(jnp.float32).astype(jnp.bfloat16), "rep", scatter_dimension=0, tiled=True
    ).astype(jnp.float32)
    global_new, moment_new = outer_update(summed, replicas, global_owned, momentum)
    rounded = global_new.astype(jnp.bfloat16)
    gathered = lax.all_gather(rounded, "rep", axis=0, tiled=True)
    returned = lax.all_to_all(gathered, "fsdp", split_axis=0, concat_axis=0, tiled=True)
    replica_params = returned.reshape(rows_here, width)
    return (global_new, moment_new, replica_params)


def solution(mesh):
    return jax.shard_map(
        body,
        mesh=mesh,
        in_specs=(P("rep", "fsdp", "tp"), P("rep", "fsdp", "tp"), P("rep", "fsdp", "tp")),
        out_specs=(P("rep", "fsdp", "tp"), P("rep", "fsdp", "tp"), P("fsdp", "tp")),
        check_vma=False,
    )
```

profile of v0, /device:TPU:25, one launch (start us, length us, event | category | flops | bytes accessed | tf_op | source)
XLA Modules:
  0.0 253.2 jit_solution(18419130461890022376)
XLA Ops:
  7.2 0.0 all-reduce.3.cloned.1.call-start
  7.2 1.3 reshape_squeeze.3
  8.6 0.5 broadcast.9
  9.1 2.2 reduce
  11.3 0.2 reshape.11
  11.4 33.4 %all_to_all.10 = bf16[16,2,4096]{2,1,0:T(2,128)(2,1)S(1)} all-to-all(bf16[16,2,4096]{2,1,0:T(2,128)(2,1)S(1)} %reshape.11), channel_id=1, replica_groups=mesh['rep'=8,'fsdp'=16,'tp'=4] {'fsdp'}, dimensions={0} | all-to-all | bytes 524288 | tf_op jit(solution)/shard_map/all_to_all | solution.py:22
  44.8 1.0 reshape.12
  45.8 0.0 copy-start
  45.8 0.0 copy-start.1
  45.8 0.0 all-reduce.3.cloned.1.call-update
  45.8 1.3 dynamic-slice
  47.8 117.3 %all-reduce.3.cloned.1.call-done = bf16[16,1,8192]{2,1,0:T(2,128)(2,1)} async-done(((bf16[16,1,8192]{2,1,0:T(2,128)(2,1)}), bf16[16,1,8192]{2,1,0:T(2,128)(2,1)}) %all-reduce.3.cloned.1.call-update) | async-done | bytes 262160
  165.1 0.0 copy-done
  165.1 0.0 copy-done.1
  165.1 1.7 fusion.2
  166.8 42.7 %all_gather.3 = bf16[16,1,8192]{2,1,0:T(2,128)(2,1)S(1)} all-gather(bf16[2,1,8192]{2,1,0:T(2,128)(2,1)S(1)} %get-tuple-element.3), channel_id=1, replica_groups=mesh['rep'=8,'fsdp'=16,'tp'=4] {'rep'}, dimensions={0}, use_global_device_ids=true | all-gather | bytes 294912 | tf_op jit(solution)/shard_map/all_gather | solution.py:28
  209.5 2.2 reduce.1
  211.6 0.2 reshape.13
  211.8 33.2 %all_to_all.11 = bf16[16,2,4096]{2,1,0:T(2,128)(2,1)S(1)} all-to-all(bf16[16,2,4096]{2,1,0:T(2,128)(2,1)S(1)} %reshape.13), channel_id=1, replica_groups=mesh['rep'=8,'fsdp'=16,'tp'=4] {'fsdp'}, dimensions={0} | all-to-all | bytes 524288 | tf_op jit(solution)/shard_map/all_to_all | solution.py:29
  245.1 0.3 reshape.14
  245.3 1.0 copy.9
Async XLA Ops:
  7.2 157.9 %all-reduce.3.cloned.1.call-start = ((), (), s32[]{:S(2)}) async-start(), calls=%async_computation.2 | async-start | bytes 1048576
  45.8 119.3 %copy-start = (f32[2,1,8192]{2,1,0:T(1,128)S(1)}, f32[2,1,8192]{2,1,0:T(1,128)}, u32[]{:S(2)}) copy-start(f32[2,1,8192]{2,1,0:T(1,128)} %param.4) | copy-start | bytes 196612
  45.8 119.3 %copy-start.1 = (f32[2,1,8192]{2,1,0:T(1,128)S(1)}, f32[2,1,8192]{2,1,0:T(1,128)}, u32[]{:S(2)}) copy-start(f32[2,1,8192]{2,1,0:T(1,128)} %param.5) | copy-start | bytes 196612
Sparse Core Ops, SparseCore 0:
  45.9 119.0 all-reduce.2
where the time goes:
time: 256 us; the launch traced here: 253 us
  waiting for transfers between devices  117 us (46%)
  blocking collectives  109 us (43%)
  between operations  14.7 us (6%)
  other arithmetic  6.05 us (2%)
  local copies, waits for them, and re-layouts  5.77 us (2%)
    unnamed x2, waiting for transfers between devices  117 us
    all_gather x1, blocking collectives, body(): gathered = lax.all_gather(rounded, 'rep', axis=0, tiled=True)  42.7 us
    all_to_all x1, blocking collectives, body(): lax.all_to_all(blocks, 'fsdp', split_axis=0, concat_axis=0, tiled=True)  33.4 us
    all_to_all x1, blocking collectives, body(): lax.all_to_all(gathered, 'fsdp', split_axis=0, concat_axis=0, tiled=True)  33.2 us
  transfers between devices with their start and end apart: 1, of which 1 were waited for; matrix products, arithmetic and copies ran while one was open for 1% of the time, Pallas kernels for 0%

commit v1 on v0

v1 whole, which is shorter than its diff:
```python
import jax
import jax.numpy as jnp
from jax import lax
from jax.sharding import PartitionSpec as P

AXES = ("rep", "fsdp")
BOTH = 8


def spot(half, quad, col, core):
    return (half * 4 + quad) * 16 + col * 2 + core


def each():
    return [(h, j, c, k) for h in range(2) for j in range(4) for c in range(8) for k in range(2)]


QUAD_CORE = [
    [spot(h, j, c, k) for j in range(4) for k in range(2)] for h in range(2) for c in range(8)
]
CROSS = [(spot(h, j, c, k), spot(1 - h, j, c, k)) for h, j, c, k in each()]
TURN = [(spot(h, j, c, k), spot(c // 4, c % 4, h * 4 + j, k)) for h, j, c, k in each()]
TURN_FLIP = [(spot(h, j, c, k), spot(1 - c // 4, c % 4, h * 4 + j, k)) for h, j, c, k in each()]


def body(local_params, global_owned, momentum):
    width = local_params.shape[2]
    half = lax.axis_index("rep") // 4
    owned = global_owned[:, 0]
    moment = momentum[:, 0]
    state = lax.reduce_precision(-0.33 * owned - 0.567 * moment, 8, 7).astype(jnp.bfloat16)

    blocks = local_params[0].reshape(2, 8, width).transpose(1, 0, 2)
    got = lax.all_to_all(blocks, AXES, split_axis=0, concat_axis=0, tiled=True, axis_index_groups=QUAD_CORE)
    part = jnp.sum(got.reshape(4, 2, 2, width).astype(jnp.float32), axis=0)
    part = lax.reduce_precision(part, 8, 7).astype(jnp.bfloat16)
    other = lax.ppermute(part, AXES, CROSS)
    state_same = lax.ppermute(state, AXES, TURN)
    state_flip = lax.ppermute(state, AXES, TURN_FLIP_A)
    summed = part.astype(jnp.float32) + other.astype(jnp.float32)
    s0 = jnp.where(half == 0, state_same, state_flip)
    s1 = jnp.where(half == 0, state_flip, state_same)
    states = jnp.stack([s0, s1], axis=1).astype(jnp.float32)
    fresh = (states + (1.33 / 8) * summed).astype(jnp.bfloat16)
    mine = jnp.where(half == 0, summed[:, 0], summed[:, 1]).astype(jnp.bfloat16)
    back = lax.ppermute(mine, AXES, TURN)

    spread = jnp.broadcast_to(fresh[None], (4, 2, 2, width)).reshape(8, 2, width)
    rows = lax.all_to_all(spread, AXES, split_axis=0, concat_axis=0, tiled=True, axis_index_groups=QUAD_CORE)
    replica_params = rows.transpose(1, 0, 2).reshape(16, width)

    mean_local = back.astype(jnp.float32) / 8
    pseudo = owned - mean_local
    moment_new = 0.9 * moment + pseudo
    global_new = owned - 0.7 * (pseudo + 0.9 * moment_new)
    return (global_new[:, None], moment_new[:, None], replica_params)


TURN_FLIP_A = [(spot(a, b, zy, k), spot(1 - zy // 4, zy % 4, a * 4 + b, k)) for a, b, zy, k in each()]


def solution(mesh):
    return jax.shard_map(
        body,
        mesh=mesh,
        in_specs=(P("rep", "fsdp", "tp"), P("rep", "fsdp", "tp"), P("rep", "fsdp", "tp")),
        out_specs=(P("rep", "fsdp", "tp"), P("rep", "fsdp", "tp"), P("fsdp", "tp")),
        check_vma=False,
    )
```

time: 256 us -> 78.5 us (0.31)
  the two profiles are of different devices: /device:TPU:25 before, /device:TPU:1 now
where the time goes in v1:
time: 78.5 us; the launch traced here: 78.1 us
  starting transfers between devices  34.7 us (44%)
  waiting for transfers between devices  19.2 us (24%)
  blocking collectives  18 us (23%)
  local copies, waits for them, and re-layouts  4.56 us (6%)
  other arithmetic  0.94 us (1%)
    all_to_all x1, blocking collectives, body(): lax.all_to_all(blocks, AXES, split_axis=0, concat_axis=0, tiled=True, axi...  18 us
    ppermute x1, starting transfers between devices, body(): state_flip = lax.ppermute(state, AXES, TURN_FLIP_A)  13.4 us
    all_to_all x1, starting transfers between devices, body(): lax.all_to_all(spread, AXES, split_axis=0, concat_axis=0, tiled=True, axi...  13.3 us
    all_to_all x1, waiting for transfers between devices, body(): lax.all_to_all(spread, AXES, split_axis=0, concat_axis=0, tiled=True, axi...  7.31 us
    ppermute x1, starting transfers between devices, body(): other = lax.ppermute(part, AXES, CROSS)  6.74 us
    ppermute x1, waiting for transfers between devices, body(): other = lax.ppermute(part, AXES, CROSS)  6.04 us
    ppermute x1, waiting for transfers between devices, body(): state_flip = lax.ppermute(state, AXES, TURN_FLIP_A)  5.82 us
  transfers between devices with their start and end apart: 5, of which 3 were waited for; matrix products, arithmetic and copies ran while one was open for 2% of the time, Pallas kernels for 0%

profile of v1, /device:TPU:1, one launch (start us, length us, event | category | flops | bytes accessed | tf_op | source)
XLA Modules:
  0.0 78.1 jit_solution(13519644626660292713)
XLA Ops:
  0.6 1.2 %copy.42 = bf16[8,2,8192]{2,1,0:T(2,128)(2,1)S(1)} copy(bf16[8,2,8192]{2,0,1:T(8,128)(2,1)} %bitcast.51) | data formatting | bytes 524288 | tf_op jit(solution)/shard_map/transpose | solution.py:33
  1.9 18.0 %all_to_all.10 = bf16[8,2,8192]{2,1,0:T(2,128)(2,1)S(1)} all-to-all(bf16[8,2,8192]{2,1,0:T(2,128)(2,1)S(1)} %copy.42), channel_id=1, replica_groups={{0,4,64,68,128,132,192,196},{8,12,72,76,136,140,200,204},{16,20,80,84,1..., dimensions={0} | all-to-all | bytes 524288 | tf_op jit(solution)/shard_map/all_to_all | solution.py:34
  19.8 0.2 convert_reduce_fusion
  20.1 6.7 %collective-permute-start = (bf16[2,2,8192]{2,1,0:T(2,128)(2,1)S(1)}, bf16[2,2,8192]{2,1,0:T(2,128)(2,1)S(1)}, u32[]{:S(2)}, u32[]{:S(2)}) collective-permute-start(bf16[2,2,8192]{2,1,0:T(2,128)(2,1)S(1)} %reduce-precision_convert_fusion), channel_id=1, source_target_pairs={{0,256},{4,260},{8,264},{12,268},{16,272},{20,276},{24,280},{28,28... | collective-permute-start | bytes 196616 | tf_op jit(solution)/shard_map/ppermute | solution.py:37
  26.9 6.0 %collective-permute-done = bf16[2,2,8192]{2,1,0:T(2,128)(2,1)S(1)} collective-permute-done((bf16[2,2,8192]{2,1,0:T(2,128)(2,1)S(1)}, bf16[2,2,8192]{2,1,0:T(2,128)(2,1)S(1)}, u32[]{:S(2)}, u32[]{:S(2)}) %collective-permute-start) | collective-permute-done | bytes 65568 | tf_op jit(solution)/shard_map/ppermute | solution.py:37
  32.9 0.1 convert_add_fusion
  33.0 0.0 copy-start.1
  33.0 0.1 fusion
  33.1 0.0 copy-start
  33.2 0.1 copy.68
  33.2 0.7 collective-permute-start.1
  33.9 0.0 collective-permute-done.1
  33.9 0.0 copy-done.1
  33.9 0.1 copy-done
  34.0 0.2 fusion.7
  34.2 13.4 %collective-permute-start.3 = (bf16[2,8192]{1,0:T(2,128)(2,1)S(1)}, bf16[2,8192]{1,0:T(2,128)(2,1)S(1)}, u32[]{:S(2)}, u32[]{:S(2)}) collective-permute-start(bf16[2,8192]{1,0:T(2,128)(2,1)S(1)} %get-tuple-element.17), channel_id=1, source_target_pairs={{0,256},{4,260},{8,320},{12,324},{16,384},{20,388},{24,448},{28,45... | collective-permute-start | bytes 98312 | tf_op jit(solution)/shard_map/ppermute | solution.py:39
  47.6 0.7 collective-permute-start.2
  48.2 5.8 %collective-permute-done.3 = bf16[2,8192]{1,0:T(2,128)(2,1)S(1)} collective-permute-done((bf16[2,8192]{1,0:T(2,128)(2,1)S(1)}, bf16[2,8192]{1,0:T(2,128)(2,1)S(1)}, u32[]{:S(2)}, u32[]{:S(2)}) %collective-permute-start.3) | collective-permute-done | bytes 32800 | tf_op jit(solution)/shard_map/ppermute | solution.py:39
  54.0 0.0 collective-permute-done.2
  54.0 0.1 fusion.5
  54.1 0.1 copy.45
  54.2 0.1 copy.46
  54.2 0.2 add_convert_fusion
  54.5 0.8 %broadcast_in_dim.14 = bf16[4,2,2,8192]{3,2,1,0:T(2,128)(2,1)} broadcast(bf16[2,2,8192]{2,1,0:T(2,128)(2,1)S(1)} %add_convert_fusion), dimensions={1,2,3} | broadcast | bytes 327680 | tf_op jit(solution)/shard_map/broadcast_in_dim | solution.py:48
  55.3 13.3 %all-to-all-start.1 = ((bf16[8,2,8192]{2,1,0:T(2,128)(2,1)}), bf16[8,2,8192]{2,1,0:T(2,128)(2,1)S(1)}, u32[]{:S(2)}, u32[]{:S(2)}) async-start(bf16[8,2,8192]{2,1,0:T(2,128)(2,1)} %bitcast.9), calls=%async_computation.1 | async-start | bytes 524288 | tf_op jit(solution)/shard_map/all_to_all | solution.py:49
  68.6 0.7 copy.49
  69.3 0.7 copy.48
  70.0 7.3 %all-to-all-done.1 = bf16[8,2,8192]{2,1,0:T(2,128)(2,1)S(1)} async-done(((bf16[8,2,8192]{2,1,0:T(2,128)(2,1)}), bf16[8,2,8192]{2,1,0:T(2,128)(2,1)S(1)}, u32[]{:S(2)}, u32[]{:S(2)}) %all-to-all-start.1) | async-done | bytes 262176 | tf_op jit(solution)/shard_map/all_to_all | solution.py:49
  77.3 0.9 %copy.67 = bf16[8,2,8192]{2,0,1:T(8,128)(2,1)} copy(bf16[8,2,8192]{2,1,0:T(2,128)(2,1)S(1)} %all-to-all-done.1) | data formatting | bytes 524288 | tf_op jit(solution)/shard_map/all_to_all | solution.py:49
  (1 shorter events, 0.0 us)
Async XLA Ops:
  20.1 12.8 %collective-permute-start = (bf16[2,2,8192]{2,1,0:T(2,128)(2,1)S(1)}, bf16[2,2,8192]{2,1,0:T(2,128)(2,1)S(1)}, u32[]{:S(2)}, u32[]{:S(2)}) collective-permute-start(bf16[2,2,8192]{2,1,0:T(2,128)(2,1)S(1)} %reduce-precision_convert_fusion), channel_id=1, source_target_pairs={{0,256},{4,260},{8,264},{12,268},{16,272},{20,276},{24,280},{28,28... | collective-permute-start | bytes 196616 | tf_op jit(solution)/shard_map/ppermute | solution.py:37
  33.0 0.9 %copy-start.1 = (f32[2,1,8192]{2,1,0:T(1,128)S(1)}, f32[2,1,8192]{2,1,0:T(1,128)}, u32[]{:S(2)}) copy-start(f32[2,1,8192]{2,1,0:T(1,128)} %param.5) | copy-start | bytes 196612
  33.1 0.8 %copy-start = (f32[2,1,8192]{2,1,0:T(1,128)S(1)}, f32[2,1,8192]{2,1,0:T(1,128)}, u32[]{:S(2)}) copy-start(f32[2,1,8192]{2,1,0:T(1,128)} %param.4) | copy-start | bytes 196612
  33.2 0.7 collective-permute-start.1
  34.2 19.9 %collective-permute-start.3 = (bf16[2,8192]{1,0:T(2,128)(2,1)S(1)}, bf16[2,8192]{1,0:T(2,128)(2,1)S(1)}, u32[]{:S(2)}, u32[]{:S(2)}) collective-permute-start(bf16[2,8192]{1,0:T(2,128)(2,1)S(1)} %get-tuple-element.17), channel_id=1, source_target_pairs={{0,256},{4,260},{8,320},{12,324},{16,384},{20,388},{24,448},{28,45... | collective-permute-start | bytes 98312 | tf_op jit(solution)/shard_map/ppermute | solution.py:39
  47.6 6.5 %collective-permute-start.2 = (bf16[2,8192]{1,0:T(2,128)(2,1)S(1)}, bf16[2,8192]{1,0:T(2,128)(2,1)S(1)}, u32[]{:S(2)}, u32[]{:S(2)}) collective-permute-start(bf16[2,8192]{1,0:T(2,128)(2,1)S(1)} %get-tuple-element.17), channel_id=1, source_target_pairs={{0,0},{4,4},{8,64},{12,68},{16,128},{20,132},{24,192},{28,196},{32... | collective-permute-start | bytes 98312 | tf_op jit(solution)/shard_map/ppermute | solution.py:38
  55.3 22.0 %all-to-all-start.1 = ((bf16[8,2,8192]{2,1,0:T(2,128)(2,1)}), bf16[8,2,8192]{2,1,0:T(2,128)(2,1)S(1)}, u32[]{:S(2)}, u32[]{:S(2)}) async-start(bf16[8,2,8192]{2,1,0:T(2,128)(2,1)} %bitcast.9), calls=%async_computation.1 | async-start | bytes 524288 | tf_op jit(solution)/shard_map/all_to_all | solution.py:49

commit v2 on v1

v2 whole, which is shorter than its diff:
```python
import jax
import jax.numpy as jnp
from jax import lax
from jax.sharding import PartitionSpec as P

AXES = ("rep", "fsdp")
SHARE = 1.33 / 8


def spot(half, quad, col, core):
    return (half * 4 + quad) * 16 + col * 2 + core


EACH = [(h, j, c, k) for h in range(2) for j in range(4) for c in range(8) for k in range(2)]
QUAD_CORE = [
    [spot(h, j, c, k) for j in range(4) for k in range(2)] for h in range(2) for c in range(8)
]
CROSS = [(spot(h, j, c, k), spot(1 - h, j, c, k)) for h, j, c, k in EACH]
TURN = [(spot(h, j, c, k), spot(c // 4, c % 4, h * 4 + j, k)) for h, j, c, k in EACH]
FLIP = [(spot(h, j, c, k), spot(1 - c // 4, c % 4, h * 4 + j, k)) for h, j, c, k in EACH]


def rounded(x):
    return lax.reduce_precision(x, 8, 7).astype(jnp.bfloat16)


def spread(x):
    return lax.all_to_all(x, AXES, split_axis=0, concat_axis=0, tiled=True, axis_index_groups=QUAD_CORE)


def body(local_params, global_owned, momentum):
    width = local_params.shape[2]
    deep = (width // 128, 128)
    half = (lax.axis_index("rep") // 4).astype(jnp.int32)
    owned = global_owned.reshape(2, *deep)
    moment = momentum.reshape(2, *deep)
    f32 = jnp.float32

    blocks = local_params[0].reshape(2, 8, *deep).transpose(1, 0, 2, 3)
    got = spread(blocks)
    state = rounded(-0.33 * owned - 0.567 * moment)
    flipped = lax.ppermute(state, AXES, FLIP).astype(f32)
    held = lax.ppermute(state, AXES, TURN).astype(f32)
    part = rounded(jnp.sum(got.reshape(4, 2, 2, *deep).astype(f32), axis=0))
    other = lax.ppermute(part, AXES, CROSS)
    total = lax.optimization_barrier(part.astype(f32) + other.astype(f32))
    here = (lax.iota(jnp.int32, 2) == half)[None, :, None, None]
    fresh = (SHARE * total + jnp.where(here, held[:, None], flipped[:, None])).astype(jnp.bfloat16)
    rows = spread(jnp.broadcast_to(fresh[None], (4, 2, 2, *deep)).reshape(8, 2, *deep))
    mine = rounded(jnp.where(half == 0, total[:, 0], total[:, 1]))
    back = lax.ppermute(mine, AXES, TURN)

    replica_params = rows.transpose(1, 0, 2, 3).reshape(16, width)
    back, owned, moment = lax.optimization_barrier((back, owned, moment))
    pseudo = owned - back.astype(f32) / 8
    moment_new = 0.9 * moment + pseudo
    global_new = owned - 0.7 * (pseudo + 0.9 * moment_new)
    return (global_new.reshape(2, 1, width), moment_new.reshape(2, 1, width), replica_params)


def solution(mesh):
    return jax.shard_map(
        body,
        mesh=mesh,
        in_specs=(P("rep", "fsdp", "tp"), P("rep", "fsdp", "tp"), P("rep", "fsdp", "tp")),
        out_specs=(P("rep", "fsdp", "tp"), P("rep", "fsdp", "tp"), P("fsdp", "tp")),
        check_vma=False,
    )
```

time: 78.5 us -> 55.4 us (0.71)
  the two profiles are of different devices: /device:TPU:1 before, /device:TPU:148 now
where the time goes in v2:
time: 55.4 us; the launch traced here: 55 us
  starting transfers between devices  35.2 us (64%)
  waiting for transfers between devices  14.8 us (27%)
  local copies, waits for them, and re-layouts  3.37 us (6%)
  other arithmetic  0.88 us (2%)
  between operations  0.76 us (1%)
    all_to_all x2, starting transfers between devices, spread(): lax.all_to_all(x, AXES, split_axis=0, concat_axis=0, tiled=True, axis_ind...  12.5 us
    ppermute x1, starting transfers between devices, body(): flipped = lax.ppermute(state, AXES, FLIP).astype(f32)  8.68 us
    ppermute x1, starting transfers between devices, body(): back = lax.ppermute(mine, AXES, TURN)  8.56 us
    ppermute x1, waiting for transfers between devices, body(): held = lax.ppermute(state, AXES, TURN).astype(f32)  7.93 us
    ppermute x1, waiting for transfers between devices, body(): back = lax.ppermute(mine, AXES, TURN)  6.34 us
    ppermute x1, starting transfers between devices, body(): other = lax.ppermute(part, AXES, CROSS)  3.55 us
    ppermute x1, starting transfers between devices, body(): held = lax.ppermute(state, AXES, TURN).astype(f32)  1.92 us
    unnamed x7, local copies, waits for them, and re-layouts  1.89 us
  transfers between devices with their start and end apart: 6, of which 3 were waited for; matrix products, arithmetic and copies ran while one was open for 1% of the time, Pallas kernels for 0%

profile of v2, /device:TPU:148, one launch (start us, length us, event | category | flops | bytes accessed | tf_op | source)
XLA Modules:
  0.0 55.0 jit_solution(7132868398961506821)
XLA Ops:
  0.6 1.0 %copy.33 = bf16[2,8,64,128]{3,2,1,0:T(8,128)(2,1)S(1)} copy(bf16[2,8,64,128]{3,1,2,0:T(8,128)(2,1)} %bitcast.29) | data formatting | bytes 524288
  1.6 0.7 %copy.20 = bf16[8,2,64,128]{3,2,1,0:T(8,128)(2,1)} copy(bf16[8,2,64,128]{3,2,0,1:T(8,128)(2,1)S(1)} %bitcast.28) | data formatting | bytes 524288 | tf_op jit(solution)/shard_map/transpose | solution.py:39
  2.4 0.0 copy-start
  2.4 0.0 copy-start.1
  2.4 6.0 %all-to-all-start = ((bf16[8,2,64,128]{3,2,1,0:T(8,128)(2,1)}), bf16[8,2,64,128]{3,2,1,0:T(8,128)(2,1)S(1)}, u32[]{:S(2)}, u32[]{:S(2)}) async-start(bf16[8,2,64,128]{3,2,1,0:T(8,128)(2,1)} %copy.20), calls=%async_computation | async-start | bytes 524288 | tf_op jit(solution)/shard_map/all_to_all | solution.py:28
  8.4 0.0 copy-done
  8.4 0.0 copy-done.1
  8.4 8.7 %collective-permute-start.3 = (bf16[2,64,128]{2,1,0:T(8,128)(2,1)S(1)}, bf16[2,64,128]{2,1,0:T(8,128)(2,1)S(1)}, u32[]{:S(2)}, u32[]{:S(2)}) collective-permute-start(bf16[2,64,128]{2,1,0:T(8,128)(2,1)S(1)} %reduce-precision_convert_fusion.1), channel_id=1, source_target_pairs={{0,256},{4,260},{8,320},{12,324},{16,384},{20,388},{24,448},{28,45... | collective-permute-start | bytes 98312 | tf_op jit(solution)/shard_map/ppermute | solution.py:42
  17.1 1.9 %collective-permute-start.2 = (bf16[2,64,128]{2,1,0:T(8,128)(2,1)S(1)}, bf16[2,64,128]{2,1,0:T(8,128)(2,1)S(1)}, u32[]{:S(2)}, u32[]{:S(2)}) collective-permute-start(bf16[2,64,128]{2,1,0:T(8,128)(2,1)S(1)} %reduce-precision_convert_fusion.1), channel_id=1, source_target_pairs={{0,0},{4,4},{8,64},{12,68},{16,128},{20,132},{24,192},{28,196},{32... | collective-permute-start | bytes 98312 | tf_op jit(solution)/shard_map/ppermute | solution.py:43
  19.1 0.5 all-to-all-done
  19.6 3.6 %collective-permute-start = (bf16[2,2,64,128]{3,2,1,0:T(8,128)(2,1)S(1)}, bf16[2,2,64,128]{3,2,1,0:T(8,128)(2,1)S(1)}, u32[]{:S(2)}, u32[]{:S(2)}) collective-permute-start(bf16[2,2,64,128]{3,2,1,0:T(8,128)(2,1)S(1)} %reduce-precision_convert_fusion), channel_id=1, source_target_pairs={{0,256},{4,260},{8,264},{12,268},{16,272},{20,276},{24,280},{28,28... | collective-permute-start | bytes 196616 | tf_op jit(solution)/shard_map/ppermute | solution.py:45
  23.2 0.0 collective-permute-done.3
  23.2 7.9 %collective-permute-done.2 = bf16[2,64,128]{2,1,0:T(8,128)(2,1)S(1)} collective-permute-done((bf16[2,64,128]{2,1,0:T(8,128)(2,1)S(1)}, bf16[2,64,128]{2,1,0:T(8,128)(2,1)S(1)}, u32[]{:S(2)}, u32[]{:S(2)}) %collective-permute-start.2) | collective-permute-done | bytes 32800 | tf_op jit(solution)/shard_map/ppermute | solution.py:43
  31.1 0.0 collective-permute-done
  31.2 0.1 add_convert_fusion
  31.3 0.8 %broadcast_in_dim.36 = bf16[4,2,2,64,128]{4,3,2,1,0:T(8,128)(2,1)} broadcast(bf16[2,2,64,128]{3,2,1,0:T(8,128)(2,1)S(1)} %add_convert_fusion), dimensions={1,2,3,4} | broadcast | bytes 327680 | tf_op jit(solution)/shard_map/broadcast_in_dim | solution.py:49
  32.0 6.4 %all-to-all-start.1 = ((bf16[8,2,64,128]{3,2,1,0:T(8,128)(2,1)}), bf16[8,2,64,128]{3,2,1,0:T(8,128)(2,1)S(1)}, u32[]{:S(2)}, u32[]{:S(2)}) async-start(bf16[8,2,64,128]{3,2,1,0:T(8,128)(2,1)} %bitcast.7), calls=%async_computation.1 | async-start | bytes 524288 | tf_op jit(solution)/shard_map/all_to_all | solution.py:28
  38.5 8.6 %collective-permute-start.1 = (bf16[2,64,128]{2,1,0:T(8,128)(2,1)S(1)}, bf16[2,64,128]{2,1,0:T(8,128)(2,1)S(1)}, u32[]{:S(2)}, u32[]{:S(2)}) collective-permute-start(bf16[2,64,128]{2,1,0:T(8,128)(2,1)S(1)} %fusion.2), channel_id=1, source_target_pairs={{0,0},{4,4},{8,64},{12,68},{16,128},{20,132},{24,192},{28,196},{32... | collective-permute-start | bytes 98312 | tf_op jit(solution)/shard_map/ppermute | solution.py:51
  47.0 6.3 %collective-permute-done.1 = bf16[2,64,128]{2,1,0:T(8,128)(2,1)S(1)} collective-permute-done((bf16[2,64,128]{2,1,0:T(8,128)(2,1)S(1)}, bf16[2,64,128]{2,1,0:T(8,128)(2,1)S(1)}, u32[]{:S(2)}, u32[]{:S(2)}) %collective-permute-start.1) | collective-permute-done | bytes 32800 | tf_op jit(solution)/shard_map/ppermute | solution.py:51
  53.4 0.7 %multiply_add_fusion = (f32[2,64,128]{2,1,0:T(8,128)}, f32[2,64,128]{2,1,0:T(8,128)}) fusion(f32[2,64,128]{2,1,0:T(8,128)S(1)} %bitcast.32, f32[2,64,128]{2,1,0:T(8,128)S(1)} %bitcast.34, bf16[2,64,128]{2,1,0:T(8,128)(2,1)S(1)} %collective-permute-done.1), kind=kLoop, calls=%fused_computation.12 | loop fusion | flops 147456 | bytes 294912 | tf_op jit(solution)/shard_map/add | solution.py:56
  54.1 0.0 all-to-all-done.1
  54.1 0.9 %copy.32 = bf16[2,8,64,128]{3,1,2,0:T(8,128)(2,1)} copy(bf16[2,8,64,128]{3,2,1,0:T(8,128)(2,1)S(1)} %copy_bitcast_fusion.1) | data formatting | bytes 524288
  (9 shorter events, 0.1 us)
Async XLA Ops:
  2.4 6.0 %copy-start = (f32[2,1,8192]{2,1,0:T(1,128)S(1)}, f32[2,1,8192]{2,1,0:T(1,128)}, u32[]{:S(2)}) copy-start(f32[2,1,8192]{2,1,0:T(1,128)} %param.5) | copy-start | bytes 196612
  2.4 6.0 %copy-start.1 = (f32[2,1,8192]{2,1,0:T(1,128)S(1)}, f32[2,1,8192]{2,1,0:T(1,128)}, u32[]{:S(2)}) copy-start(f32[2,1,8192]{2,1,0:T(1,128)} %param.4) | copy-start | bytes 196612
  2.4 17.2 %all-to-all-start = ((bf16[8,2,64,128]{3,2,1,0:T(8,128)(2,1)}), bf16[8,2,64,128]{3,2,1,0:T(8,128)(2,1)S(1)}, u32[]{:S(2)}, u32[]{:S(2)}) async-start(bf16[8,2,64,128]{3,2,1,0:T(8,128)(2,1)} %copy.20), calls=%async_computation | async-start | bytes 524288 | tf_op jit(solution)/shard_map/all_to_all | solution.py:28
  8.4 14.8 %collective-permute-start.3 = (bf16[2,64,128]{2,1,0:T(8,128)(2,1)S(1)}, bf16[2,64,128]{2,1,0:T(8,128)(2,1)S(1)}, u32[]{:S(2)}, u32[]{:S(2)}) collective-permute-start(bf16[2,64,128]{2,1,0:T(8,128)(2,1)S(1)} %reduce-precision_convert_fusion.1), channel_id=1, source_target_pairs={{0,256},{4,260},{8,320},{12,324},{16,384},{20,388},{24,448},{28,45... | collective-permute-start | bytes 98312 | tf_op jit(solution)/shard_map/ppermute | solution.py:42
  17.1 14.0 %collective-permute-start.2 = (bf16[2,64,128]{2,1,0:T(8,128)(2,1)S(1)}, bf16[2,64,128]{2,1,0:T(8,128)(2,1)S(1)}, u32[]{:S(2)}, u32[]{:S(2)}) collective-permute-start(bf16[2,64,128]{2,1,0:T(8,128)(2,1)S(1)} %reduce-precision_convert_fusion.1), channel_id=1, source_target_pairs={{0,0},{4,4},{8,64},{12,68},{16,128},{20,132},{24,192},{28,196},{32... | collective-permute-start | bytes 98312 | tf_op jit(solution)/shard_map/ppermute | solution.py:43
  19.6 11.5 %collective-permute-start = (bf16[2,2,64,128]{3,2,1,0:T(8,128)(2,1)S(1)}, bf16[2,2,64,128]{3,2,1,0:T(8,128)(2,1)S(1)}, u32[]{:S(2)}, u32[]{:S(2)}) collective-permute-start(bf16[2,2,64,128]{3,2,1,0:T(8,128)(2,1)S(1)} %reduce-precision_convert_fusion), channel_id=1, source_target_pairs={{0,256},{4,260},{8,264},{12,268},{16,272},{20,276},{24,280},{28,28... | collective-permute-start | bytes 196616 | tf_op jit(solution)/shard_map/ppermute | solution.py:45
  32.0 22.0 %all-to-all-start.1 = ((bf16[8,2,64,128]{3,2,1,0:T(8,128)(2,1)}), bf16[8,2,64,128]{3,2,1,0:T(8,128)(2,1)S(1)}, u32[]{:S(2)}, u32[]{:S(2)}) async-start(bf16[8,2,64,128]{3,2,1,0:T(8,128)(2,1)} %bitcast.7), calls=%async_computation.1 | async-start | bytes 524288 | tf_op jit(solution)/shard_map/all_to_all | solution.py:28
  38.5 14.9 %collective-permute-start.1 = (bf16[2,64,128]{2,1,0:T(8,128)(2,1)S(1)}, bf16[2,64,128]{2,1,0:T(8,128)(2,1)S(1)}, u32[]{:S(2)}, u32[]{:S(2)}) collective-permute-start(bf16[2,64,128]{2,1,0:T(8,128)(2,1)S(1)} %fusion.2), channel_id=1, source_target_pairs={{0,0},{4,4},{8,64},{12,68},{16,128},{20,132},{24,192},{28,196},{32... | collective-permute-start | bytes 98312 | tf_op jit(solution)/shard_map/ppermute | solution.py:51

commit v3 on v2

v3 whole, which is shorter than its diff:
```python
import jax
import jax.numpy as jnp
from jax import lax
from jax.sharding import PartitionSpec as P

AXES = ("rep", "fsdp")
SHARE = 1.33 / 8


def spot(rep, col, core):
    return rep * 16 + col * 2 + core


EACH = [(b, c, k) for b in range(8) for c in range(8) for k in range(2)]
LINE = [
    [spot(r, c, k) for y in range(4) for r in (4 + y, 3 - y) for k in range(2)] for c in range(8)
]
HOLDER = [3 - b if b < 4 else b for b in range(8)]
TO_HOLDER = [(spot(c, b, k), spot(HOLDER[b], c, k)) for b, c, k in EACH]
TO_OWNER = [(b, a) for a, b in TO_HOLDER]


def rounded(x):
    return lax.reduce_precision(x, 8, 7).astype(jnp.bfloat16)


def swap_rows(x):
    return lax.all_to_all(x, AXES, split_axis=0, concat_axis=0, tiled=True, axis_index_groups=LINE)


def body(local_params, global_owned, momentum):
    rows, width = local_params.shape[1:]
    deep = (width // 128, 128)
    owned = global_owned.reshape(2, *deep)
    moment = momentum.reshape(2, *deep)
    f32 = jnp.float32

    blocks = local_params[0].reshape(2, 4, 2, *deep)[::-1].transpose(1, 0, 2, 3, 4)
    got = swap_rows(blocks.reshape(rows, *deep))
    state = rounded(-0.33 * owned - 0.567 * moment)
    held = lax.ppermute(state, AXES, TO_HOLDER).astype(f32)
    summed = jnp.sum(got.reshape(8, 2, *deep).astype(f32), axis=0)
    fresh = (held + SHARE * summed).astype(jnp.bfloat16)
    back = lax.ppermute(rounded(summed), AXES, TO_OWNER)
    spread = jnp.broadcast_to(fresh[None], (8, 2, *deep)).reshape(rows, *deep)
    out = swap_rows(spread).reshape(4, 2, 2, *deep).transpose(1, 0, 2, 3, 4)[::-1]
    replica_params = out.reshape(rows, width)

    back, owned, moment = lax.optimization_barrier((back, owned, moment))
    pseudo = owned - back.astype(f32) / 8
    moment_new = 0.9 * moment + pseudo
    global_new = owned - 0.7 * (pseudo + 0.9 * moment_new)
    return (global_new.reshape(2, 1, width), moment_new.reshape(2, 1, width), replica_params)


def solution(mesh):
    return jax.shard_map(
        body,
        mesh=mesh,
        in_specs=(P("rep", "fsdp", "tp"), P("rep", "fsdp", "tp"), P("rep", "fsdp", "tp")),
        out_specs=(P("rep", "fsdp", "tp"), P("rep", "fsdp", "tp"), P("fsdp", "tp")),
        check_vma=False,
    )
```

time: 55.4 us -> 54 us (0.975)
  the two profiles are of different devices: /device:TPU:148 before, /device:TPU:1 now
where the time goes in v3:
time: 54 us; the launch traced here: 53.6 us
  starting transfers between devices  29.7 us (55%)
  waiting for transfers between devices  19 us (35%)
  local copies, waits for them, and re-layouts  3.41 us (6%)
  other arithmetic  0.75 us (1%)
  between operations  0.71 us (1%)
    all_to_all x2, starting transfers between devices, swap_rows(): lax.all_to_all(x, AXES, split_axis=0, concat_axis=0, tiled=True, axis_ind...  21.7 us
    all_to_all x2, waiting for transfers between devices, swap_rows(): lax.all_to_all(x, AXES, split_axis=0, concat_axis=0, tiled=True, axis_ind...  12.8 us
    ppermute x1, waiting for transfers between devices, body(): back = lax.ppermute(rounded(summed), AXES, TO_OWNER)  6.26 us
    ppermute x1, starting transfers between devices, body(): back = lax.ppermute(rounded(summed), AXES, TO_OWNER)  5.77 us
    ppermute x1, starting transfers between devices, body(): held = lax.ppermute(state, AXES, TO_HOLDER).astype(f32)  2.19 us
    unnamed x6, local copies, waits for them, and re-layouts  1.88 us
  transfers between devices with their start and end apart: 4, of which 3 were waited for; matrix products, arithmetic and copies ran while one was open for 1% of the time, Pallas kernels for 0%

profile of v3, /device:TPU:1, one launch (start us, length us, event | category | flops | bytes accessed | tf_op | source)
XLA Modules:
  0.0 53.6 jit_solution(12808005624424556444)
XLA Ops:
  0.6 1.0 %copy.8 = bf16[2,8,64,128]{3,2,1,0:T(8,128)(2,1)S(1)} copy(bf16[2,8,64,128]{3,1,2,0:T(8,128)(2,1)} %bitcast.26) | data formatting | bytes 524288
  1.7 0.7 %copy.6 = bf16[4,2,2,64,128]{4,3,2,1,0:T(8,128)(2,1)} copy(bf16[4,2,2,64,128]{4,3,2,0,1:T(8,128)(2,1)S(1)} %reverse_bitcast_fusion) | data formatting | bytes 524288 | tf_op jit(solution)/shard_map/transpose | solution.py:38
  2.4 0.0 copy-start
  2.4 0.0 copy-start.1
  2.4 14.4 %all-to-all-start = ((bf16[16,64,128]{2,1,0:T(8,128)(2,1)}), bf16[16,64,128]{2,1,0:T(8,128)(2,1)S(1)}, u32[]{:S(2)}, u32[]{:S(2)}) async-start(bf16[16,64,128]{2,1,0:T(8,128)(2,1)} %bitcast.1), calls=%async_computation | async-start | bytes 524288 | tf_op jit(solution)/shard_map/all_to_all | solution.py:28
  16.8 0.0 copy-done
  16.8 0.0 copy-done.1
  16.8 2.2 %collective-permute-start.1 = (bf16[2,64,128]{2,1,0:T(8,128)(2,1)S(1)}, bf16[2,64,128]{2,1,0:T(8,128)(2,1)S(1)}, u32[]{:S(2)}, u32[]{:S(2)}) collective-permute-start(bf16[2,64,128]{2,1,0:T(8,128)(2,1)S(1)} %reduce-precision_convert_fusion), channel_id=1, source_target_pairs={{0,192},{4,196},{64,200},{68,204},{128,208},{132,212},{192,216},{1... | collective-permute-start | bytes 98312 | tf_op jit(solution)/shard_map/ppermute | solution.py:41
  19.0 11.7 %all-to-all-done = bf16[16,64,128]{2,1,0:T(8,128)(2,1)S(1)} async-done(((bf16[16,64,128]{2,1,0:T(8,128)(2,1)}), bf16[16,64,128]{2,1,0:T(8,128)(2,1)S(1)}, u32[]{:S(2)}, u32[]{:S(2)}) %all-to-all-start) | async-done | bytes 262176 | tf_op jit(solution)/shard_map/all_to_all | solution.py:28
  30.7 0.0 collective-permute-done.1
  30.8 0.8 %broadcast_in_dim.2 = bf16[8,2,64,128]{3,2,1,0:T(8,128)(2,1)} broadcast(bf16[2,64,128]{2,1,0:T(8,128)(2,1)S(1)} %get-tuple-element.11), dimensions={1,2,3} | broadcast | bytes 294912 | tf_op jit(solution)/shard_map/broadcast_in_dim | solution.py:45
  31.5 7.3 %all-to-all-start.1 = ((bf16[16,64,128]{2,1,0:T(8,128)(2,1)}), bf16[16,64,128]{2,1,0:T(8,128)(2,1)S(1)}, u32[]{:S(2)}, u32[]{:S(2)}) async-start(bf16[16,64,128]{2,1,0:T(8,128)(2,1)} %bitcast.7), calls=%async_computation.1 | async-start | bytes 524288 | tf_op jit(solution)/shard_map/all_to_all | solution.py:28
  38.9 5.8 %collective-permute-start = (bf16[2,64,128]{2,1,0:T(8,128)(2,1)S(1)}, bf16[2,64,128]{2,1,0:T(8,128)(2,1)S(1)}, u32[]{:S(2)}, u32[]{:S(2)}) collective-permute-start(bf16[2,64,128]{2,1,0:T(8,128)(2,1)S(1)} %get-tuple-element.12), channel_id=1, source_target_pairs={{192,0},{196,4},{200,64},{204,68},{208,128},{212,132},{216,192},{2... | collective-permute-start | bytes 98312 | tf_op jit(solution)/shard_map/ppermute | solution.py:44
  44.7 6.3 %collective-permute-done = bf16[2,64,128]{2,1,0:T(8,128)(2,1)S(1)} collective-permute-done((bf16[2,64,128]{2,1,0:T(8,128)(2,1)S(1)}, bf16[2,64,128]{2,1,0:T(8,128)(2,1)S(1)}, u32[]{:S(2)}, u32[]{:S(2)}) %collective-permute-start) | collective-permute-done | bytes 32800 | tf_op jit(solution)/shard_map/ppermute | solution.py:44
  50.9 0.7 %multiply_add_fusion = (f32[2,64,128]{2,1,0:T(8,128)}, f32[2,64,128]{2,1,0:T(8,128)}) fusion(f32[2,64,128]{2,1,0:T(8,128)S(1)} %bitcast.29, f32[2,64,128]{2,1,0:T(8,128)S(1)} %bitcast.31, bf16[2,64,128]{2,1,0:T(8,128)(2,1)S(1)} %collective-permute-done), kind=kLoop, calls=%fused_computation.6 | loop fusion | flops 147456 | bytes 294912 | tf_op jit(solution)/shard_map/add | solution.py:51
  51.6 1.1 %all-to-all-done.1 = bf16[16,64,128]{2,1,0:T(8,128)(2,1)S(1)} async-done(((bf16[16,64,128]{2,1,0:T(8,128)(2,1)}), bf16[16,64,128]{2,1,0:T(8,128)(2,1)S(1)}, u32[]{:S(2)}, u32[]{:S(2)}) %all-to-all-start.1) | async-done | bytes 262176 | tf_op jit(solution)/shard_map/all_to_all | solution.py:28
  52.7 0.9 %copy.11 = bf16[2,8,64,128]{3,1,2,0:T(8,128)(2,1)} copy(bf16[2,8,64,128]{3,2,1,0:T(8,128)(2,1)S(1)} %bitcast.24) | data formatting | bytes 524288
  (6 shorter events, 0.1 us)
Async XLA Ops:
  2.4 14.4 %copy-start = (f32[2,1,8192]{2,1,0:T(1,128)S(1)}, f32[2,1,8192]{2,1,0:T(1,128)}, u32[]{:S(2)}) copy-start(f32[2,1,8192]{2,1,0:T(1,128)} %param.5) | copy-start | bytes 196612
  2.4 14.4 %copy-start.1 = (f32[2,1,8192]{2,1,0:T(1,128)S(1)}, f32[2,1,8192]{2,1,0:T(1,128)}, u32[]{:S(2)}) copy-start(f32[2,1,8192]{2,1,0:T(1,128)} %param.4) | copy-start | bytes 196612
  2.4 28.3 %all-to-all-start = ((bf16[16,64,128]{2,1,0:T(8,128)(2,1)}), bf16[16,64,128]{2,1,0:T(8,128)(2,1)S(1)}, u32[]{:S(2)}, u32[]{:S(2)}) async-start(bf16[16,64,128]{2,1,0:T(8,128)(2,1)} %bitcast.1), calls=%async_computation | async-start | bytes 524288 | tf_op jit(solution)/shard_map/all_to_all | solution.py:28
  16.8 13.9 %collective-permute-start.1 = (bf16[2,64,128]{2,1,0:T(8,128)(2,1)S(1)}, bf16[2,64,128]{2,1,0:T(8,128)(2,1)S(1)}, u32[]{:S(2)}, u32[]{:S(2)}) collective-permute-start(bf16[2,64,128]{2,1,0:T(8,128)(2,1)S(1)} %reduce-precision_convert_fusion), channel_id=1, source_target_pairs={{0,192},{4,196},{64,200},{68,204},{128,208},{132,212},{192,216},{1... | collective-permute-start | bytes 98312 | tf_op jit(solution)/shard_map/ppermute | solution.py:41
  31.5 21.1 %all-to-all-start.1 = ((bf16[16,64,128]{2,1,0:T(8,128)(2,1)}), bf16[16,64,128]{2,1,0:T(8,128)(2,1)S(1)}, u32[]{:S(2)}, u32[]{:S(2)}) async-start(bf16[16,64,128]{2,1,0:T(8,128)(2,1)} %bitcast.7), calls=%async_computation.1 | async-start | bytes 524288 | tf_op jit(solution)/shard_map/all_to_all | solution.py:28
  38.9 12.0 %collective-permute-start = (bf16[2,64,128]{2,1,0:T(8,128)(2,1)S(1)}, bf16[2,64,128]{2,1,0:T(8,128)(2,1)S(1)}, u32[]{:S(2)}, u32[]{:S(2)}) collective-permute-start(bf16[2,64,128]{2,1,0:T(8,128)(2,1)S(1)} %get-tuple-element.12), channel_id=1, source_target_pairs={{192,0},{196,4},{200,64},{204,68},{208,128},{212,132},{216,192},{2... | collective-permute-start | bytes 98312 | tf_op jit(solution)/shard_map/ppermute | solution.py:44

commit v4 on v3

--- a/solution.py
+++ b/solution.py
@@ -5,18 +5,26 @@
 
 AXES = ("rep", "fsdp")
 SHARE = 1.33 / 8
+UPPER = ((4, 7, 5, 6), (4, 5, 6, 7))
+LOWER = (((0, 3, 2, 1), (3, 2, 1, 0)), ((3, 2, 1, 0), (0, 1, 2, 3)))
 
 
 def spot(rep, col, core):
     return rep * 16 + col * 2 + core
 
 
-EACH = [(b, c, k) for b in range(8) for c in range(8) for k in range(2)]
+def holder(block, col, core):
+    side = col // 4
+    rep = UPPER[side][block - 4] if block >= 4 else LOWER[side][core][block]
+    return spot(rep, col, core)
+
+
 LINE = [
-    [spot(r, c, k) for y in range(4) for r in (4 + y, 3 - y) for k in range(2)] for c in range(8)
+    [holder(block, c, k) for y in range(4) for block in (4 + y, y) for k in (1, 0)] for c in range(8)
 ]
-HOLDER = [3 - b if b < 4 else b for b in range(8)]
-TO_HOLDER = [(spot(c, b, k), spot(HOLDER[b], c, k)) for b, c, k in EACH]
+TO_HOLDER = [
+    (spot(c, block, k), holder(block, c, k)) for block in range(8) for c in range(8) for k in range(2)
+]
 TO_OWNER = [(b, a) for a, b in TO_HOLDER]
 
 
@@ -35,15 +43,15 @@
     moment = momentum.reshape(2, *deep)
     f32 = jnp.float32
 
-    blocks = local_params[0].reshape(2, 4, 2, *deep)[::-1].transpose(1, 0, 2, 3, 4)
+    blocks = local_params[0].reshape(2, 4, 2, *deep)[::-1, :, ::-1].transpose(1, 0, 2, 3, 4)
     got = swap_rows(blocks.reshape(rows, *deep))
     state = rounded(-0.33 * owned - 0.567 * moment)
     held = lax.ppermute(state, AXES, TO_HOLDER).astype(f32)
-    summed = jnp.sum(got.reshape(8, 2, *deep).astype(f32), axis=0)
+    summed = jnp.sum(got.reshape(8, 2, *deep).astype(f32), axis=0)[::-1]
     fresh = (held + SHARE * summed).astype(jnp.bfloat16)
     back = lax.ppermute(rounded(summed), AXES, TO_OWNER)
-    spread = jnp.broadcast_to(fresh[None], (8, 2, *deep)).reshape(rows, *deep)
-    out = swap_rows(spread).reshape(4, 2, 2, *deep).transpose(1, 0, 2, 3, 4)[::-1]
+    spread = jnp.broadcast_to(fresh[None, ::-1], (8, 2, *deep)).reshape(rows, *deep)
+    out = swap_rows(spread).reshape(4, 2, 2, *deep).transpose(1, 0, 2, 3, 4)[::-1, :, ::-1]
     replica_params = out.reshape(rows, width)
 
     back, owned, moment = lax.optimization_barrier((back, owned, moment))

time: 54 us -> 52.2 us (0.967)
  the two profiles are of different devices: /device:TPU:1 before, /device:TPU:25 now
where the time goes in v4:
time: 52.2 us; the launch traced here: 51.2 us
  starting transfers between devices  27 us (52%)
  waiting for transfers between devices  19.3 us (37%)
  local copies, waits for them, and re-layouts  3.41 us (7%)
  other arithmetic  0.75 us (1%)
  between operations  0.72 us (1%)
    all_to_all x2, starting transfers between devices, swap_rows(): lax.all_to_all(x, AXES, split_axis=0, concat_axis=0, tiled=True, axis_ind...  22.9 us
    all_to_all x2, waiting for transfers between devices, swap_rows(): lax.all_to_all(x, AXES, split_axis=0, concat_axis=0, tiled=True, axis_ind...  15.3 us
    ppermute x1, waiting for transfers between devices, body(): back = lax.ppermute(rounded(summed), AXES, TO_OWNER)  4 us
    ppermute x1, starting transfers between devices, body(): back = lax.ppermute(rounded(summed), AXES, TO_OWNER)  2.15 us
    ppermute x1, starting transfers between devices, body(): held = lax.ppermute(state, AXES, TO_HOLDER).astype(f32)  1.92 us
    unnamed x6, local copies, waits for them, and re-layouts  1.88 us
  transfers between devices with their start and end apart: 4, of which 3 were waited for; matrix products, arithmetic and copies ran while one was open for 1% of the time, Pallas kernels for 0%

profile of v4, /device:TPU:25, one launch (start us, length us, event | category | flops | bytes accessed | tf_op | source)
XLA Modules:
  0.0 51.2 jit_solution(1955868625844768749)
XLA Ops:
  0.6 1.0 %copy.8 = bf16[2,8,64,128]{3,2,1,0:T(8,128)(2,1)S(1)} copy(bf16[2,8,64,128]{3,1,2,0:T(8,128)(2,1)} %bitcast.26) | data formatting | bytes 524288
  1.7 0.7 %copy.6 = bf16[4,2,2,64,128]{4,3,2,1,0:T(8,128)(2,1)} copy(bf16[4,2,2,64,128]{4,3,2,0,1:T(8,128)(2,1)S(1)} %reverse_bitcast_fusion) | data formatting | bytes 524288 | tf_op jit(solution)/shard_map/transpose | solution.py:46
  2.4 0.0 copy-start
  2.4 0.0 copy-start.1
  2.4 13.3 %all-to-all-start = ((bf16[16,64,128]{2,1,0:T(8,128)(2,1)}), bf16[16,64,128]{2,1,0:T(8,128)(2,1)S(1)}, u32[]{:S(2)}, u32[]{:S(2)}) async-start(bf16[16,64,128]{2,1,0:T(8,128)(2,1)} %bitcast.1), calls=%async_computation | async-start | bytes 524288 | tf_op jit(solution)/shard_map/all_to_all | solution.py:36
  15.7 0.0 copy-done
  15.7 0.0 copy-done.1
  15.7 1.9 %collective-permute-start.1 = (bf16[2,64,128]{2,1,0:T(8,128)(2,1)S(1)}, bf16[2,64,128]{2,1,0:T(8,128)(2,1)S(1)}, u32[]{:S(2)}, u32[]{:S(2)}) collective-permute-start(bf16[2,64,128]{2,1,0:T(8,128)(2,1)S(1)} %reduce-precision_convert_fusion), channel_id=1, source_target_pairs={{0,0},{4,196},{64,8},{68,204},{128,16},{132,212},{192,24},{196,220... | collective-permute-start | bytes 98312 | tf_op jit(solution)/shard_map/ppermute | solution.py:49
  17.6 10.0 %all-to-all-done = bf16[16,64,128]{2,1,0:T(8,128)(2,1)S(1)} async-done(((bf16[16,64,128]{2,1,0:T(8,128)(2,1)}), bf16[16,64,128]{2,1,0:T(8,128)(2,1)S(1)}, u32[]{:S(2)}, u32[]{:S(2)}) %all-to-all-start) | async-done | bytes 262176 | tf_op jit(solution)/shard_map/all_to_all | solution.py:36
  27.7 0.0 collective-permute-done.1
  27.7 0.8 %broadcast_in_dim.2 = bf16[8,2,64,128]{3,2,1,0:T(8,128)(2,1)} broadcast(bf16[2,64,128]{2,1,0:T(8,128)(2,1)S(1)} %rev.14), dimensions={1,2,3} | broadcast | bytes 294912 | tf_op jit(solution)/shard_map/broadcast_in_dim | solution.py:53
  28.5 9.7 %all-to-all-start.1 = ((bf16[16,64,128]{2,1,0:T(8,128)(2,1)}), bf16[16,64,128]{2,1,0:T(8,128)(2,1)S(1)}, u32[]{:S(2)}, u32[]{:S(2)}) async-start(bf16[16,64,128]{2,1,0:T(8,128)(2,1)} %bitcast.7), calls=%async_computation.1 | async-start | bytes 524288 | tf_op jit(solution)/shard_map/all_to_all | solution.py:36
  38.1 2.1 %collective-permute-start = (bf16[2,64,128]{2,1,0:T(8,128)(2,1)S(1)}, bf16[2,64,128]{2,1,0:T(8,128)(2,1)S(1)}, u32[]{:S(2)}, u32[]{:S(2)}) collective-permute-start(bf16[2,64,128]{2,1,0:T(8,128)(2,1)S(1)} %get-tuple-element.12), channel_id=1, source_target_pairs={{0,0},{196,4},{8,64},{204,68},{16,128},{212,132},{24,192},{220,196... | collective-permute-start | bytes 98312 | tf_op jit(solution)/shard_map/ppermute | solution.py:52
  40.3 4.0 %collective-permute-done = bf16[2,64,128]{2,1,0:T(8,128)(2,1)S(1)} collective-permute-done((bf16[2,64,128]{2,1,0:T(8,128)(2,1)S(1)}, bf16[2,64,128]{2,1,0:T(8,128)(2,1)S(1)}, u32[]{:S(2)}, u32[]{:S(2)}) %collective-permute-start) | collective-permute-done | bytes 32800 | tf_op jit(solution)/shard_map/ppermute | solution.py:52
  44.3 0.7 %multiply_add_fusion = (f32[2,64,128]{2,1,0:T(8,128)}, f32[2,64,128]{2,1,0:T(8,128)}) fusion(f32[2,64,128]{2,1,0:T(8,128)S(1)} %bitcast.29, f32[2,64,128]{2,1,0:T(8,128)S(1)} %bitcast.31, bf16[2,64,128]{2,1,0:T(8,128)(2,1)S(1)} %collective-permute-done), kind=kLoop, calls=%fused_computation.6 | loop fusion | flops 147456 | bytes 294912 | tf_op jit(solution)/shard_map/add | solution.py:59
  45.0 5.3 %all-to-all-done.1 = bf16[16,64,128]{2,1,0:T(8,128)(2,1)S(1)} async-done(((bf16[16,64,128]{2,1,0:T(8,128)(2,1)}), bf16[16,64,128]{2,1,0:T(8,128)(2,1)S(1)}, u32[]{:S(2)}, u32[]{:S(2)}) %all-to-all-start.1) | async-done | bytes 262176 | tf_op jit(solution)/shard_map/all_to_all | solution.py:36
  50.3 0.9 %copy.11 = bf16[2,8,64,128]{3,1,2,0:T(8,128)(2,1)} copy(bf16[2,8,64,128]{3,2,1,0:T(8,128)(2,1)S(1)} %bitcast.24) | data formatting | bytes 524288
  (7 shorter events, 0.1 us)
Async XLA Ops:
  2.4 13.3 %copy-start = (f32[2,1,8192]{2,1,0:T(1,128)S(1)}, f32[2,1,8192]{2,1,0:T(1,128)}, u32[]{:S(2)}) copy-start(f32[2,1,8192]{2,1,0:T(1,128)} %param.5) | copy-start | bytes 196612
  2.4 13.3 %copy-start.1 = (f32[2,1,8192]{2,1,0:T(1,128)S(1)}, f32[2,1,8192]{2,1,0:T(1,128)}, u32[]{:S(2)}) copy-start(f32[2,1,8192]{2,1,0:T(1,128)} %param.4) | copy-start | bytes 196612
  2.4 25.2 %all-to-all-start = ((bf16[16,64,128]{2,1,0:T(8,128)(2,1)}), bf16[16,64,128]{2,1,0:T(8,128)(2,1)S(1)}, u32[]{:S(2)}, u32[]{:S(2)}) async-start(bf16[16,64,128]{2,1,0:T(8,128)(2,1)} %bitcast.1), calls=%async_computation | async-start | bytes 524288 | tf_op jit(solution)/shard_map/all_to_all | solution.py:36
  15.7 12.0 %collective-permute-start.1 = (bf16[2,64,128]{2,1,0:T(8,128)(2,1)S(1)}, bf16[2,64,128]{2,1,0:T(8,128)(2,1)S(1)}, u32[]{:S(2)}, u32[]{:S(2)}) collective-permute-start(bf16[2,64,128]{2,1,0:T(8,128)(2,1)S(1)} %reduce-precision_convert_fusion), channel_id=1, source_target_pairs={{0,0},{4,196},{64,8},{68,204},{128,16},{132,212},{192,24},{196,220... | collective-permute-start | bytes 98312 | tf_op jit(solution)/shard_map/ppermute | solution.py:49
  28.5 21.8 %all-to-all-start.1 = ((bf16[16,64,128]{2,1,0:T(8,128)(2,1)}), bf16[16,64,128]{2,1,0:T(8,128)(2,1)S(1)}, u32[]{:S(2)}, u32[]{:S(2)}) async-start(bf16[16,64,128]{2,1,0:T(8,128)(2,1)} %bitcast.7), calls=%async_computation.1 | async-start | bytes 524288 | tf_op jit(solution)/shard_map/all_to_all | solution.py:36
  38.1 6.2 %collective-permute-start = (bf16[2,64,128]{2,1,0:T(8,128)(2,1)S(1)}, bf16[2,64,128]{2,1,0:T(8,128)(2,1)S(1)}, u32[]{:S(2)}, u32[]{:S(2)}) collective-permute-start(bf16[2,64,128]{2,1,0:T(8,128)(2,1)S(1)} %get-tuple-element.12), channel_id=1, source_target_pairs={{0,0},{196,4},{8,64},{204,68},{16,128},{212,132},{24,192},{220,196... | collective-permute-start | bytes 98312 | tf_op jit(solution)/shard_map/ppermute | solution.py:52

commit v5 on v4

--- a/solution.py
+++ b/solution.py
@@ -1,6 +1,8 @@
 import jax
 import jax.numpy as jnp
 from jax import lax
+from jax.experimental import pallas as pl
+from jax.experimental.pallas import tpu as pltpu
 from jax.sharding import PartitionSpec as P
 
 AXES = ("rep", "fsdp")
@@ -36,6 +38,31 @@
     return lax.all_to_all(x, AXES, split_axis=0, concat_axis=0, tiled=True, axis_index_groups=LINE)
 
 
+def fresh_kernel(got_ref, held_ref, spread_ref, sums_ref):
+    f32 = jnp.float32
+    for core in range(2):
+        summed = got_ref[0, 1 - core].astype(f32)
+        for i in range(1, 8):
+            summed = summed + got_ref[i, 1 - core].astype(f32)
+        sums_ref[core] = summed.astype(jnp.bfloat16)
+        fresh = (held_ref[core].astype(f32) + SHARE * summed).astype(jnp.bfloat16)
+        for i in range(8):
+            spread_ref[i, 1 - core] = fresh
+
+
+def fresh_rows(got, held):
+    vmem = pl.BlockSpec(memory_space=pltpu.VMEM)
+    got = pltpu.with_memory_space_constraint(got, pltpu.VMEM)
+    held = pltpu.with_memory_space_constraint(held, pltpu.VMEM)
+    return pl.pallas_call(
+        fresh_kernel,
+        out_shape=[pltpu.VMEM(got.shape, got.dtype), pltpu.VMEM(held.shape, held.dtype)],
+        in_specs=[vmem] * 2,
+        out_specs=[vmem] * 2,
+        compiler_params=pltpu.CompilerParams(vmem_limit_bytes=4 * 2**20),
+    )(got, held)
+
+
 def body(local_params, global_owned, momentum):
     rows, width = local_params.shape[1:]
     deep = (width // 128, 128)
@@ -46,11 +73,10 @@
     blocks = local_params[0].reshape(2, 4, 2, *deep)[::-1, :, ::-1].transpose(1, 0, 2, 3, 4)
     got = swap_rows(blocks.reshape(rows, *deep))
     state = rounded(-0.33 * owned - 0.567 * moment)
-    held = lax.ppermute(state, AXES, TO_HOLDER).astype(f32)
-    summed = jnp.sum(got.reshape(8, 2, *deep).astype(f32), axis=0)[::-1]
-    fresh = (held + SHARE * summed).astype(jnp.bfloat16)
-    back = lax.ppermute(rounded(summed), AXES, TO_OWNER)
-    spread = jnp.broadcast_to(fresh[None, ::-1], (8, 2, *deep)).reshape(rows, *deep)
+    held = lax.ppermute(state, AXES, TO_HOLDER)
+    spread, sums = fresh_rows(got.reshape(8, 2, *deep), held)
+    back = lax.ppermute(sums, AXES, TO_OWNER)
+    spread = spread.reshape(rows, *deep)
     out = swap_rows(spread).reshape(4, 2, 2, *deep).transpose(1, 0, 2, 3, 4)[::-1, :, ::-1]
     replica_params = out.reshape(rows, width)
 

time: 52.2 us -> 52.2 us (level)
  local copies, waits for them, and re-layouts: 3.41 us -> 2.65 us
  Pallas kernels: 0 us -> 0.75 us
    all_to_all x2, waiting for transfers between devices: 15.3 us -> 6.47 us  [swap_rows(): lax.all_to_all(x, AXES, split_axis=0, concat_axis=0, tiled=True, axis_ind...]
    ppermute x2, waiting for transfers between devices: 4 us -> 12.8 us  [the longest x1 8.84 us: body(): held = lax.ppermute(state, AXES, TO_HOLDER)]
    broadcast_in_dim x1 -> x0, local copies, waits for them, and re-layouts: 0.75 us -> none  [body(): jnp.broadcast_to(fresh[None, ::-1], (8, 2, *deep)).reshape(rows, *deep)]
    pallas_call x0 -> x1, Pallas kernels: none -> 0.75 us  [fresh_rows(): pl.pallas_call(fresh_kernel, out_shape=[pltpu.VMEM(got.shape, got.dtype),...]
  transfers between devices with their start and end apart: 4 -> 4, of which waited for: 3 -> 4; matrix products, arithmetic and copies ran while one was open for 1% -> 1% of each run, Pallas kernels for 0% -> 0%
where the time goes in v5:
time: 52.2 us; the launch traced here: 51.2 us
  starting transfers between devices  27.1 us (52%)
  waiting for transfers between devices  19.3 us (37%)
  local copies, waits for them, and re-layouts  2.65 us (5%)
  Pallas kernels  0.75 us (1%)
  between operations  0.7 us (1%)
  other arithmetic  0.69 us (1%)
    all_to_all x2, starting transfers between devices, swap_rows(): lax.all_to_all(x, AXES, split_axis=0, concat_axis=0, tiled=True, axis_ind...  23 us
    ppermute x1, waiting for transfers between devices, body(): held = lax.ppermute(state, AXES, TO_HOLDER)  8.84 us
    all_to_all x2, waiting for transfers between devices, swap_rows(): lax.all_to_all(x, AXES, split_axis=0, concat_axis=0, tiled=True, axis_ind...  6.47 us
    ppermute x1, waiting for transfers between devices, body(): back = lax.ppermute(sums, AXES, TO_OWNER)  4 us
    ppermute x1, starting transfers between devices, body(): back = lax.ppermute(sums, AXES, TO_OWNER)  2.15 us
    ppermute x1, starting transfers between devices, body(): held = lax.ppermute(state, AXES, TO_HOLDER)  1.92 us
    unnamed x6, local copies, waits for them, and re-layouts  1.88 us
  transfers between devices with their start and end apart: 4, of which 4 were waited for; matrix products, arithmetic and copies ran while one was open for 1% of the time, Pallas kernels for 0%

profile of v5, /device:TPU:25, one launch (start us, length us, event | category | flops | bytes accessed | tf_op | source)
XLA Modules:
  0.0 51.2 jit_solution(16628748176967507191)
XLA Ops:
  0.6 1.0 %copy.10 = bf16[2,8,64,128]{3,2,1,0:T(8,128)(2,1)S(1)} copy(bf16[2,8,64,128]{3,1,2,0:T(8,128)(2,1)} %bitcast.27) | data formatting | bytes 524288
  1.7 0.7 %copy.6 = bf16[4,2,2,64,128]{4,3,2,1,0:T(8,128)(2,1)} copy(bf16[4,2,2,64,128]{4,3,2,0,1:T(8,128)(2,1)S(1)} %reverse_bitcast_fusion) | data formatting | bytes 524288 | tf_op jit(solution)/shard_map/transpose | solution.py:73
  2.4 0.0 copy-start
  2.4 0.0 copy-start.1
  2.4 13.3 %all-to-all-start = ((bf16[16,64,128]{2,1,0:T(8,128)(2,1)}), bf16[16,64,128]{2,1,0:T(8,128)(2,1)S(1)}, u32[]{:S(2)}, u32[]{:S(2)}) async-start(bf16[16,64,128]{2,1,0:T(8,128)(2,1)} %bitcast.1), calls=%async_computation | async-start | bytes 524288 | tf_op jit(solution)/shard_map/all_to_all | solution.py:38
  15.7 0.0 copy-done
  15.7 0.0 copy-done.1
  15.7 1.9 %collective-permute-start = (bf16[2,64,128]{2,1,0:T(8,128)(2,1)S(1)}, bf16[2,64,128]{2,1,0:T(8,128)(2,1)S(1)}, u32[]{:S(2)}, u32[]{:S(2)}) collective-permute-start(bf16[2,64,128]{2,1,0:T(8,128)(2,1)S(1)} %reduce-precision_convert_fusion), channel_id=1, source_target_pairs={{0,0},{4,196},{64,8},{68,204},{128,16},{132,212},{192,24},{196,220... | collective-permute-start | bytes 98312 | tf_op jit(solution)/shard_map/ppermute | solution.py:76
  17.6 8.8 %collective-permute-done.held_ref = bf16[2,64,128]{2,1,0:T(8,128)(2,1)S(1)} collective-permute-done((bf16[2,64,128]{2,1,0:T(8,128)(2,1)S(1)}, bf16[2,64,128]{2,1,0:T(8,128)(2,1)S(1)}, u32[]{:S(2)}, u32[]{:S(2)}) %collective-permute-start) | collective-permute-done | bytes 32800 | tf_op jit(solution)/shard_map/ppermute | solution.py:76
  26.5 1.2 %all-to-all-done = bf16[16,64,128]{2,1,0:T(8,128)(2,1)S(1)} async-done(((bf16[16,64,128]{2,1,0:T(8,128)(2,1)}), bf16[16,64,128]{2,1,0:T(8,128)(2,1)S(1)}, u32[]{:S(2)}, u32[]{:S(2)}) %all-to-all-start) | async-done | bytes 262176 | tf_op jit(solution)/shard_map/all_to_all | solution.py:38
  27.6 0.8 %shard_map.58 = (bf16[8,2,64,128]{3,2,1,0:T(8,128)(2,1)}, bf16[2,64,128]{2,1,0:T(8,128)(2,1)S(1)}) custom-call(bf16[8,2,64,128]{3,2,1,0:T(8,128)(2,1)S(1)} %bitcast.22, bf16[2,64,128]{2,1,0:T(8,128)(2,1)S(1)} %collective-permute-done.held_ref), custom_call_target="tpu_custom_call" | custom-call | tf_op jit(solution)/shard_map/pallas_call | solution.py:57
  28.4 9.7 %all-to-all-start.1 = ((bf16[16,64,128]{2,1,0:T(8,128)(2,1)}), bf16[16,64,128]{2,1,0:T(8,128)(2,1)S(1)}, u32[]{:S(2)}, u32[]{:S(2)}) async-start(bf16[16,64,128]{2,1,0:T(8,128)(2,1)} %bitcast.7), calls=%async_computation.1 | async-start | bytes 524288 | tf_op jit(solution)/shard_map/all_to_all | solution.py:38
  38.1 2.1 %collective-permute-start.1 = (bf16[2,64,128]{2,1,0:T(8,128)(2,1)S(1)}, bf16[2,64,128]{2,1,0:T(8,128)(2,1)S(1)}, u32[]{:S(2)}, u32[]{:S(2)}) collective-permute-start(bf16[2,64,128]{2,1,0:T(8,128)(2,1)S(1)} %get-tuple-element.8), channel_id=1, source_target_pairs={{0,0},{196,4},{8,64},{204,68},{16,128},{212,132},{24,192},{220,196... | collective-permute-start | bytes 98312 | tf_op jit(solution)/shard_map/ppermute | solution.py:78
  40.3 4.0 %collective-permute-done.1 = bf16[2,64,128]{2,1,0:T(8,128)(2,1)S(1)} collective-permute-done((bf16[2,64,128]{2,1,0:T(8,128)(2,1)S(1)}, bf16[2,64,128]{2,1,0:T(8,128)(2,1)S(1)}, u32[]{:S(2)}, u32[]{:S(2)}) %collective-permute-start.1) | collective-permute-done | bytes 32800 | tf_op jit(solution)/shard_map/ppermute | solution.py:78
  44.3 0.7 %multiply_add_fusion = (f32[2,64,128]{2,1,0:T(8,128)}, f32[2,64,128]{2,1,0:T(8,128)}) fusion(f32[2,64,128]{2,1,0:T(8,128)S(1)} %bitcast.30, f32[2,64,128]{2,1,0:T(8,128)S(1)} %bitcast.32, bf16[2,64,128]{2,1,0:T(8,128)(2,1)S(1)} %collective-permute-done.1), kind=kLoop, calls=%fused_computation.4 | loop fusion | flops 147456 | bytes 294912 | tf_op jit(solution)/shard_map/add | solution.py:85
  44.9 5.3 %all-to-all-done.1 = bf16[16,64,128]{2,1,0:T(8,128)(2,1)S(1)} async-done(((bf16[16,64,128]{2,1,0:T(8,128)(2,1)}), bf16[16,64,128]{2,1,0:T(8,128)(2,1)S(1)}, u32[]{:S(2)}, u32[]{:S(2)}) %all-to-all-start.1) | async-done | bytes 262176 | tf_op jit(solution)/shard_map/all_to_all | solution.py:38
  50.3 0.9 %copy.14 = bf16[2,8,64,128]{3,1,2,0:T(8,128)(2,1)} copy(bf16[2,8,64,128]{3,2,1,0:T(8,128)(2,1)S(1)} %bitcast.25) | data formatting | bytes 524288
  (4 shorter events, 0.1 us)
Async XLA Ops:
  2.4 13.3 %copy-start = (f32[2,1,8192]{2,1,0:T(1,128)S(1)}, f32[2,1,8192]{2,1,0:T(1,128)}, u32[]{:S(2)}) copy-start(f32[2,1,8192]{2,1,0:T(1,128)} %param.5) | copy-start | bytes 196612
  2.4 13.3 %copy-start.1 = (f32[2,1,8192]{2,1,0:T(1,128)S(1)}, f32[2,1,8192]{2,1,0:T(1,128)}, u32[]{:S(2)}) copy-start(f32[2,1,8192]{2,1,0:T(1,128)} %param.4) | copy-start | bytes 196612
  2.4 25.2 %all-to-all-start = ((bf16[16,64,128]{2,1,0:T(8,128)(2,1)}), bf16[16,64,128]{2,1,0:T(8,128)(2,1)S(1)}, u32[]{:S(2)}, u32[]{:S(2)}) async-start(bf16[16,64,128]{2,1,0:T(8,128)(2,1)} %bitcast.1), calls=%async_computation | async-start | bytes 524288 | tf_op jit(solution)/shard_map/all_to_all | solution.py:38
  15.7 10.8 %collective-permute-start = (bf16[2,64,128]{2,1,0:T(8,128)(2,1)S(1)}, bf16[2,64,128]{2,1,0:T(8,128)(2,1)S(1)}, u32[]{:S(2)}, u32[]{:S(2)}) collective-permute-start(bf16[2,64,128]{2,1,0:T(8,128)(2,1)S(1)} %reduce-precision_convert_fusion), channel_id=1, source_target_pairs={{0,0},{4,196},{64,8},{68,204},{128,16},{132,212},{192,24},{196,220... | collective-permute-start | bytes 98312 | tf_op jit(solution)/shard_map/ppermute | solution.py:76
  28.4 21.9 %all-to-all-start.1 = ((bf16[16,64,128]{2,1,0:T(8,128)(2,1)}), bf16[16,64,128]{2,1,0:T(8,128)(2,1)S(1)}, u32[]{:S(2)}, u32[]{:S(2)}) async-start(bf16[16,64,128]{2,1,0:T(8,128)(2,1)} %bitcast.7), calls=%async_computation.1 | async-start | bytes 524288 | tf_op jit(solution)/shard_map/all_to_all | solution.py:38
  38.1 6.2 %collective-permute-start.1 = (bf16[2,64,128]{2,1,0:T(8,128)(2,1)S(1)}, bf16[2,64,128]{2,1,0:T(8,128)(2,1)S(1)}, u32[]{:S(2)}, u32[]{:S(2)}) collective-permute-start(bf16[2,64,128]{2,1,0:T(8,128)(2,1)S(1)} %get-tuple-element.8), channel_id=1, source_target_pairs={{0,0},{196,4},{8,64},{204,68},{16,128},{212,132},{24,192},{220,196... | collective-permute-start | bytes 98312 | tf_op jit(solution)/shard_map/ppermute | solution.py:78

commit v6 on v5

--- a/solution.py
+++ b/solution.py
@@ -38,6 +38,83 @@
     return lax.all_to_all(x, AXES, split_axis=0, concat_axis=0, tiled=True, axis_index_groups=LINE)
 
 
+LISTED = [(4 * upper + y) * 2 + core for y in range(4) for upper in (1, 0) for core in (1, 0)]
+
+
+PIECES = 4
+
+
+def listed_kernel(rows_ref, out_ref, taken, listed, in_sems, out_sems):
+    wide = rows_ref.shape[1] // PIECES
+    deep = out_ref.shape[1] // PIECES
+    fetches = [
+        pltpu.make_async_copy(rows_ref.at[:, pl.ds(i * wide, wide)], taken.at[i], in_sems.at[i])
+        for i in range(PIECES)
+    ]
+    stores = [
+        pltpu.make_async_copy(listed.at[i], out_ref.at[:, pl.ds(i * deep, deep), :], out_sems.at[i])
+        for i in range(PIECES)
+    ]
+    for fetch in fetches:
+        fetch.start()
+    for i in range(PIECES):
+        fetches[i].wait()
+        rows = taken[i].reshape(rows_ref.shape[0], deep, 128)
+        for place, row in enumerate(LISTED):
+            listed[i, place] = rows[row]
+        stores[i].start()
+    for store in stores:
+        store.wait()
+
+
+def listed_rows(rows, deep):
+    anywhere = pl.BlockSpec(memory_space=pl.ANY)
+    count, width = rows.shape
+    return pl.pallas_call(
+        listed_kernel,
+        out_shape=jax.ShapeDtypeStruct((count,) + deep, rows.dtype),
+        in_specs=[anywhere],
+        out_specs=anywhere,
+        scratch_shapes=[
+            pltpu.VMEM((PIECES, count, width // PIECES), rows.dtype),
+            pltpu.VMEM((PIECES, count, deep[0] // PIECES, 128), rows.dtype),
+            pltpu.SemaphoreType.DMA((PIECES,)),
+            pltpu.SemaphoreType.DMA((PIECES,)),
+        ],
+    )(rows)
+
+
+def plain_kernel(listed_ref, out_ref, plain, sems):
+    wide = out_ref.shape[1] // PIECES
+    deep = listed_ref.shape[1] // PIECES
+    stores = []
+    for i in range(PIECES):
+        rows = [listed_ref[LISTED.index(row), i * deep : (i + 1) * deep] for row in range(len(LISTED))]
+        plain[i] = jnp.stack(rows).reshape(len(LISTED), wide)
+        stores.append(
+            pltpu.make_async_copy(plain.at[i], out_ref.at[:, pl.ds(i * wide, wide)], sems.at[i])
+        )
+        stores[-1].start()
+    for store in stores:
+        store.wait()
+
+
+def plain_rows(listed):
+    count, deep, _ = listed.shape
+    listed = pltpu.with_memory_space_constraint(listed, pltpu.VMEM)
+    return pl.pallas_call(
+        plain_kernel,
+        out_shape=jax.ShapeDtypeStruct((count, deep * 128), listed.dtype),
+        in_specs=[pl.BlockSpec(memory_space=pltpu.VMEM)],
+        out_specs=pl.BlockSpec(memory_space=pl.ANY),
+        scratch_shapes=[
+            pltpu.VMEM((PIECES, count, deep * 128 // PIECES), listed.dtype),
+            pltpu.SemaphoreType.DMA((PIECES,)),
+        ],
+        compiler_params=pltpu.CompilerParams(vmem_limit_bytes=4 * 2**20),
+    )(listed)
+
+
 def fresh_kernel(got_ref, held_ref, spread_ref, sums_ref):
     f32 = jnp.float32
     for core in range(2):
@@ -70,15 +147,13 @@
     moment = momentum.reshape(2, *deep)
     f32 = jnp.float32
 
-    blocks = local_params[0].reshape(2, 4, 2, *deep)[::-1, :, ::-1].transpose(1, 0, 2, 3, 4)
-    got = swap_rows(blocks.reshape(rows, *deep))
+    got = swap_rows(listed_rows(local_params[0], deep))
     state = rounded(-0.33 * owned - 0.567 * moment)
     held = lax.ppermute(state, AXES, TO_HOLDER)
     spread, sums = fresh_rows(got.reshape(8, 2, *deep), held)
     back = lax.ppermute(sums, AXES, TO_OWNER)
     spread = spread.reshape(rows, *deep)
-    out = swap_rows(spread).reshape(4, 2, 2, *deep).transpose(1, 0, 2, 3, 4)[::-1, :, ::-1]
-    replica_params = out.reshape(rows, width)
+    replica_params = plain_rows(swap_rows(spread))
 
     back, owned, moment = lax.optimization_barrier((back, owned, moment))
     pseudo = owned - back.astype(f32) / 8

time: 52.2 us -> 52 us (level)
  local copies, waits for them, and re-layouts: 2.65 us -> 0.01 us
  Pallas kernels: 0.75 us -> 3.17 us
    pallas_call x0 -> x2, Pallas kernels: none -> 2.41 us  [the longest x1 1.66 us: listed_rows(): pl.pallas_call(listed_kernel, out_shape=jax.ShapeDtypeStruct((count,) + d...]
    unnamed x6 -> x4, local copies, waits for them, and re-layouts: 1.88 us -> 0.01 us
    transpose x2 -> x0, local copies, waits for them, and re-layouts: 0.74 us -> none  [body(): local_params[0].reshape(2, 4, 2, *deep)[::-1, :, ::-1]]
where the time goes in v6:
time: 52 us; the launch traced here: 50.9 us
  starting transfers between devices  27.1 us (52%)
  waiting for transfers between devices  19.3 us (37%)
  Pallas kernels  3.17 us (6%)
  other arithmetic  0.69 us (1%)
  between operations  0.69 us (1%)
    all_to_all x2, starting transfers between devices, swap_rows(): lax.all_to_all(x, AXES, split_axis=0, concat_axis=0, tiled=True, axis_ind...  23 us
    ppermute x1, waiting for transfers between devices, body(): held = lax.ppermute(state, AXES, TO_HOLDER)  8.84 us
    all_to_all x2, waiting for transfers between devices, swap_rows(): lax.all_to_all(x, AXES, split_axis=0, concat_axis=0, tiled=True, axis_ind...  6.47 us
    ppermute x1, waiting for transfers between devices, body(): back = lax.ppermute(sums, AXES, TO_OWNER)  4 us
    ppermute x1, starting transfers between devices, body(): back = lax.ppermute(sums, AXES, TO_OWNER)  2.15 us
    ppermute x1, starting transfers between devices, body(): held = lax.ppermute(state, AXES, TO_HOLDER)  1.92 us
    pallas_call x1, Pallas kernels, listed_rows(): pl.pallas_call(listed_kernel, out_shape=jax.ShapeDtypeStruct((count,) + d...  1.66 us
  transfers between devices with their start and end apart: 4, of which 4 were waited for; matrix products, arithmetic and copies ran while one was open for 1% of the time, Pallas kernels for 0%

profile of v6, /device:TPU:25, one launch (start us, length us, event | category | flops | bytes accessed | tf_op | source)
XLA Modules:
  0.0 50.9 jit_solution(16445639487441652264)
XLA Ops:
  0.6 1.7 %shard_map.58 = bf16[16,64,128]{2,1,0:T(8,128)(2,1)} custom-call(bf16[16,8192]{1,0:T(8,128)(2,1)} %bitcast.8), custom_call_target="tpu_custom_call" | custom-call | tf_op jit(solution)/shard_map/pallas_call | solution.py:73
  2.3 0.0 copy-start
  2.3 0.0 copy-start.1
  2.3 13.3 %all-to-all-start = ((bf16[16,64,128]{2,1,0:T(8,128)(2,1)}), bf16[16,64,128]{2,1,0:T(8,128)(2,1)S(1)}, u32[]{:S(2)}, u32[]{:S(2)}) async-start(bf16[16,64,128]{2,1,0:T(8,128)(2,1)} %shard_map.58), calls=%async_computation | async-start | bytes 524288 | tf_op jit(solution)/shard_map/all_to_all | solution.py:38
  15.6 0.0 copy-done
  15.6 0.0 copy-done.1
  15.6 1.9 %collective-permute-start = (bf16[2,64,128]{2,1,0:T(8,128)(2,1)S(1)}, bf16[2,64,128]{2,1,0:T(8,128)(2,1)S(1)}, u32[]{:S(2)}, u32[]{:S(2)}) collective-permute-start(bf16[2,64,128]{2,1,0:T(8,128)(2,1)S(1)} %reduce-precision_convert_fusion), channel_id=1, source_target_pairs={{0,0},{4,196},{64,8},{68,204},{128,16},{132,212},{192,24},{196,220... | collective-permute-start | bytes 98312 | tf_op jit(solution)/shard_map/ppermute | solution.py:152
  17.6 8.8 %collective-permute-done.held_ref = bf16[2,64,128]{2,1,0:T(8,128)(2,1)S(1)} collective-permute-done((bf16[2,64,128]{2,1,0:T(8,128)(2,1)S(1)}, bf16[2,64,128]{2,1,0:T(8,128)(2,1)S(1)}, u32[]{:S(2)}, u32[]{:S(2)}) %collective-permute-start) | collective-permute-done | bytes 32800 | tf_op jit(solution)/shard_map/ppermute | solution.py:152
  26.4 1.2 %all-to-all-done = bf16[16,64,128]{2,1,0:T(8,128)(2,1)S(1)} async-done(((bf16[16,64,128]{2,1,0:T(8,128)(2,1)}), bf16[16,64,128]{2,1,0:T(8,128)(2,1)S(1)}, u32[]{:S(2)}, u32[]{:S(2)}) %all-to-all-start) | async-done | bytes 262176 | tf_op jit(solution)/shard_map/all_to_all | solution.py:38
  27.6 0.8 %shard_map.59 = (bf16[8,2,64,128]{3,2,1,0:T(8,128)(2,1)}, bf16[2,64,128]{2,1,0:T(8,128)(2,1)S(1)}) custom-call(bf16[8,2,64,128]{3,2,1,0:T(8,128)(2,1)S(1)} %bitcast.7, bf16[2,64,128]{2,1,0:T(8,128)(2,1)S(1)} %collective-permute-done.held_ref), custom_call_target="tpu_custom_call" | custom-call | tf_op jit(solution)/shard_map/pallas_call | solution.py:134
  28.3 9.7 %all-to-all-start.1 = ((bf16[16,64,128]{2,1,0:T(8,128)(2,1)}), bf16[16,64,128]{2,1,0:T(8,128)(2,1)S(1)}, u32[]{:S(2)}, u32[]{:S(2)}) async-start(bf16[16,64,128]{2,1,0:T(8,128)(2,1)} %bitcast.6), calls=%async_computation.1 | async-start | bytes 524288 | tf_op jit(solution)/shard_map/all_to_all | solution.py:38
  38.1 2.1 %collective-permute-start.1 = (bf16[2,64,128]{2,1,0:T(8,128)(2,1)S(1)}, bf16[2,64,128]{2,1,0:T(8,128)(2,1)S(1)}, u32[]{:S(2)}, u32[]{:S(2)}) collective-permute-start(bf16[2,64,128]{2,1,0:T(8,128)(2,1)S(1)} %get-tuple-element.8), channel_id=1, source_target_pairs={{0,0},{196,4},{8,64},{204,68},{16,128},{212,132},{24,192},{220,196... | collective-permute-start | bytes 98312 | tf_op jit(solution)/shard_map/ppermute | solution.py:154
  40.2 4.0 %collective-permute-done.1 = bf16[2,64,128]{2,1,0:T(8,128)(2,1)S(1)} collective-permute-done((bf16[2,64,128]{2,1,0:T(8,128)(2,1)S(1)}, bf16[2,64,128]{2,1,0:T(8,128)(2,1)S(1)}, u32[]{:S(2)}, u32[]{:S(2)}) %collective-permute-start.1) | collective-permute-done | bytes 32800 | tf_op jit(solution)/shard_map/ppermute | solution.py:154
  44.2 0.7 %multiply_add_fusion = (f32[2,64,128]{2,1,0:T(8,128)}, f32[2,64,128]{2,1,0:T(8,128)}) fusion(f32[2,64,128]{2,1,0:T(8,128)S(1)} %bitcast.10, f32[2,64,128]{2,1,0:T(8,128)S(1)} %bitcast.12, bf16[2,64,128]{2,1,0:T(8,128)(2,1)S(1)} %collective-permute-done.1), kind=kLoop, calls=%fused_computation.1 | loop fusion | flops 147456 | bytes 294912 | tf_op jit(solution)/shard_map/add | solution.py:160
  44.9 5.3 %all-to-all-done.1.listed_ref = bf16[16,64,128]{2,1,0:T(8,128)(2,1)S(1)} async-done(((bf16[16,64,128]{2,1,0:T(8,128)(2,1)}), bf16[16,64,128]{2,1,0:T(8,128)(2,1)S(1)}, u32[]{:S(2)}, u32[]{:S(2)}) %all-to-all-start.1) | async-done | bytes 262176 | tf_op jit(solution)/shard_map/all_to_all | solution.py:38
  50.2 0.8 %shard_map.60 = bf16[16,8192]{1,0:T(8,128)(2,1)} custom-call(bf16[16,64,128]{2,1,0:T(8,128)(2,1)S(1)} %all-to-all-done.1.listed_ref), custom_call_target="tpu_custom_call" | custom-call | tf_op jit(solution)/shard_map/pallas_call | solution.py:105
  (1 shorter events, 0.0 us)
Async XLA Ops:
  2.3 13.3 %copy-start = (f32[2,1,8192]{2,1,0:T(1,128)S(1)}, f32[2,1,8192]{2,1,0:T(1,128)}, u32[]{:S(2)}) copy-start(f32[2,1,8192]{2,1,0:T(1,128)} %param.5) | copy-start | bytes 196612
  2.3 13.3 %copy-start.1 = (f32[2,1,8192]{2,1,0:T(1,128)S(1)}, f32[2,1,8192]{2,1,0:T(1,128)}, u32[]{:S(2)}) copy-start(f32[2,1,8192]{2,1,0:T(1,128)} %param.4) | copy-start | bytes 196612
  2.3 25.3 %all-to-all-start = ((bf16[16,64,128]{2,1,0:T(8,128)(2,1)}), bf16[16,64,128]{2,1,0:T(8,128)(2,1)S(1)}, u32[]{:S(2)}, u32[]{:S(2)}) async-start(bf16[16,64,128]{2,1,0:T(8,128)(2,1)} %shard_map.58), calls=%async_computation | async-start | bytes 524288 | tf_op jit(solution)/shard_map/all_to_all | solution.py:38
  15.6 10.8 %collective-permute-start = (bf16[2,64,128]{2,1,0:T(8,128)(2,1)S(1)}, bf16[2,64,128]{2,1,0:T(8,128)(2,1)S(1)}, u32[]{:S(2)}, u32[]{:S(2)}) collective-permute-start(bf16[2,64,128]{2,1,0:T(8,128)(2,1)S(1)} %reduce-precision_convert_fusion), channel_id=1, source_target_pairs={{0,0},{4,196},{64,8},{68,204},{128,16},{132,212},{192,24},{196,220... | collective-permute-start | bytes 98312 | tf_op jit(solution)/shard_map/ppermute | solution.py:152
  28.3 21.9 %all-to-all-start.1 = ((bf16[16,64,128]{2,1,0:T(8,128)(2,1)}), bf16[16,64,128]{2,1,0:T(8,128)(2,1)S(1)}, u32[]{:S(2)}, u32[]{:S(2)}) async-start(bf16[16,64,128]{2,1,0:T(8,128)(2,1)} %bitcast.6), calls=%async_computation.1 | async-start | bytes 524288 | tf_op jit(solution)/shard_map/all_to_all | solution.py:38
  38.1 6.2 %collective-permute-start.1 = (bf16[2,64,128]{2,1,0:T(8,128)(2,1)S(1)}, bf16[2,64,128]{2,1,0:T(8,128)(2,1)S(1)}, u32[]{:S(2)}, u32[]{:S(2)}) collective-permute-start(bf16[2,64,128]{2,1,0:T(8,128)(2,1)S(1)} %get-tuple-element.8), channel_id=1, source_target_pairs={{0,0},{196,4},{8,64},{204,68},{16,128},{212,132},{24,192},{220,196... | collective-permute-start | bytes 98312 | tf_op jit(solution)/shard_map/ppermute | solution.py:154

commit v7 on v6

--- a/solution.py
+++ b/solution.py
@@ -8,7 +8,7 @@
 AXES = ("rep", "fsdp")
 SHARE = 1.33 / 8
 UPPER = ((4, 7, 5, 6), (4, 5, 6, 7))
-LOWER = (((0, 3, 2, 1), (3, 2, 1, 0)), ((3, 2, 1, 0), (0, 1, 2, 3)))
+LOWER = (((0, 3, 2, 1), (3, 1, 2, 0)), ((3, 2, 1, 0), (0, 1, 2, 3)))
 
 
 def spot(rep, col, core):

time: 52 us -> 51.5 us (level)
  no operation moved by 1% of the time
where the time goes in v7:
time: 51.5 us; the launch traced here: 50.9 us
  starting transfers between devices  27.1 us (53%)
  waiting for transfers between devices  19.3 us (37%)
  Pallas kernels  3.17 us (6%)
  other arithmetic  0.69 us (1%)
  between operations  0.69 us (1%)
    all_to_all x2, starting transfers between devices, swap_rows(): lax.all_to_all(x, AXES, split_axis=0, concat_axis=0, tiled=True, axis_ind...  23 us
    ppermute x1, waiting for transfers between devices, body(): held = lax.ppermute(state, AXES, TO_HOLDER)  8.84 us
    all_to_all x2, waiting for transfers between devices, swap_rows(): lax.all_to_all(x, AXES, split_axis=0, concat_axis=0, tiled=True, axis_ind...  6.47 us
    ppermute x1, waiting for transfers between devices, body(): back = lax.ppermute(sums, AXES, TO_OWNER)  4 us
    ppermute x1, starting transfers between devices, body(): back = lax.ppermute(sums, AXES, TO_OWNER)  2.15 us
    ppermute x1, starting transfers between devices, body(): held = lax.ppermute(state, AXES, TO_HOLDER)  1.92 us
    pallas_call x1, Pallas kernels, listed_rows(): pl.pallas_call(listed_kernel, out_shape=jax.ShapeDtypeStruct((count,) + d...  1.66 us
  transfers between devices with their start and end apart: 4, of which 4 were waited for; matrix products, arithmetic and copies ran while one was open for 1% of the time, Pallas kernels for 0%

profile of v7, /device:TPU:25, one launch (start us, length us, event | category | flops | bytes accessed | tf_op | source)
XLA Modules:
  0.0 50.9 jit_solution(3047670099662235150)
XLA Ops:
  0.6 1.7 %shard_map.58 = bf16[16,64,128]{2,1,0:T(8,128)(2,1)} custom-call(bf16[16,8192]{1,0:T(8,128)(2,1)} %bitcast.8), custom_call_target="tpu_custom_call" | custom-call | tf_op jit(solution)/shard_map/pallas_call | solution.py:73
  2.3 0.0 copy-start
  2.3 0.0 copy-start.1
  2.3 13.3 %all-to-all-start = ((bf16[16,64,128]{2,1,0:T(8,128)(2,1)}), bf16[16,64,128]{2,1,0:T(8,128)(2,1)S(1)}, u32[]{:S(2)}, u32[]{:S(2)}) async-start(bf16[16,64,128]{2,1,0:T(8,128)(2,1)} %shard_map.58), calls=%async_computation | async-start | bytes 524288 | tf_op jit(solution)/shard_map/all_to_all | solution.py:38
  15.6 0.0 copy-done
  15.6 0.0 copy-done.1
  15.6 1.9 %collective-permute-start = (bf16[2,64,128]{2,1,0:T(8,128)(2,1)S(1)}, bf16[2,64,128]{2,1,0:T(8,128)(2,1)S(1)}, u32[]{:S(2)}, u32[]{:S(2)}) collective-permute-start(bf16[2,64,128]{2,1,0:T(8,128)(2,1)S(1)} %reduce-precision_convert_fusion), channel_id=1, source_target_pairs={{0,0},{4,196},{64,8},{68,204},{128,16},{132,212},{192,24},{196,220... | collective-permute-start | bytes 98312 | tf_op jit(solution)/shard_map/ppermute | solution.py:152
  17.6 8.8 %collective-permute-done.held_ref = bf16[2,64,128]{2,1,0:T(8,128)(2,1)S(1)} collective-permute-done((bf16[2,64,128]{2,1,0:T(8,128)(2,1)S(1)}, bf16[2,64,128]{2,1,0:T(8,128)(2,1)S(1)}, u32[]{:S(2)}, u32[]{:S(2)}) %collective-permute-start) | collective-permute-done | bytes 32800 | tf_op jit(solution)/shard_map/ppermute | solution.py:152
  26.4 1.2 %all-to-all-done = bf16[16,64,128]{2,1,0:T(8,128)(2,1)S(1)} async-done(((bf16[16,64,128]{2,1,0:T(8,128)(2,1)}), bf16[16,64,128]{2,1,0:T(8,128)(2,1)S(1)}, u32[]{:S(2)}, u32[]{:S(2)}) %all-to-all-start) | async-done | bytes 262176 | tf_op jit(solution)/shard_map/all_to_all | solution.py:38
  27.6 0.8 %shard_map.59 = (bf16[8,2,64,128]{3,2,1,0:T(8,128)(2,1)}, bf16[2,64,128]{2,1,0:T(8,128)(2,1)S(1)}) custom-call(bf16[8,2,64,128]{3,2,1,0:T(8,128)(2,1)S(1)} %bitcast.7, bf16[2,64,128]{2,1,0:T(8,128)(2,1)S(1)} %collective-permute-done.held_ref), custom_call_target="tpu_custom_call" | custom-call | tf_op jit(solution)/shard_map/pallas_call | solution.py:134
  28.3 9.7 %all-to-all-start.1 = ((bf16[16,64,128]{2,1,0:T(8,128)(2,1)}), bf16[16,64,128]{2,1,0:T(8,128)(2,1)S(1)}, u32[]{:S(2)}, u32[]{:S(2)}) async-start(bf16[16,64,128]{2,1,0:T(8,128)(2,1)} %bitcast.6), calls=%async_computation.1 | async-start | bytes 524288 | tf_op jit(solution)/shard_map/all_to_all | solution.py:38
  38.1 2.1 %collective-permute-start.1 = (bf16[2,64,128]{2,1,0:T(8,128)(2,1)S(1)}, bf16[2,64,128]{2,1,0:T(8,128)(2,1)S(1)}, u32[]{:S(2)}, u32[]{:S(2)}) collective-permute-start(bf16[2,64,128]{2,1,0:T(8,128)(2,1)S(1)} %get-tuple-element.8), channel_id=1, source_target_pairs={{0,0},{196,4},{8,64},{204,68},{16,128},{212,132},{24,192},{220,196... | collective-permute-start | bytes 98312 | tf_op jit(solution)/shard_map/ppermute | solution.py:154
  40.2 4.0 %collective-permute-done.1 = bf16[2,64,128]{2,1,0:T(8,128)(2,1)S(1)} collective-permute-done((bf16[2,64,128]{2,1,0:T(8,128)(2,1)S(1)}, bf16[2,64,128]{2,1,0:T(8,128)(2,1)S(1)}, u32[]{:S(2)}, u32[]{:S(2)}) %collective-permute-start.1) | collective-permute-done | bytes 32800 | tf_op jit(solution)/shard_map/ppermute | solution.py:154
  44.2 0.7 %multiply_add_fusion = (f32[2,64,128]{2,1,0:T(8,128)}, f32[2,64,128]{2,1,0:T(8,128)}) fusion(f32[2,64,128]{2,1,0:T(8,128)S(1)} %bitcast.10, f32[2,64,128]{2,1,0:T(8,128)S(1)} %bitcast.12, bf16[2,64,128]{2,1,0:T(8,128)(2,1)S(1)} %collective-permute-done.1), kind=kLoop, calls=%fused_computation.1 | loop fusion | flops 147456 | bytes 294912 | tf_op jit(solution)/shard_map/add | solution.py:160
  44.9 5.3 %all-to-all-done.1.listed_ref = bf16[16,64,128]{2,1,0:T(8,128)(2,1)S(1)} async-done(((bf16[16,64,128]{2,1,0:T(8,128)(2,1)}), bf16[16,64,128]{2,1,0:T(8,128)(2,1)S(1)}, u32[]{:S(2)}, u32[]{:S(2)}) %all-to-all-start.1) | async-done | bytes 262176 | tf_op jit(solution)/shard_map/all_to_all | solution.py:38
  50.2 0.8 %shard_map.60 = bf16[16,8192]{1,0:T(8,128)(2,1)} custom-call(bf16[16,64,128]{2,1,0:T(8,128)(2,1)S(1)} %all-to-all-done.1.listed_ref), custom_call_target="tpu_custom_call" | custom-call | tf_op jit(solution)/shard_map/pallas_call | solution.py:105
  (1 shorter events, 0.0 us)
Async XLA Ops:
  2.3 13.3 %copy-start = (f32[2,1,8192]{2,1,0:T(1,128)S(1)}, f32[2,1,8192]{2,1,0:T(1,128)}, u32[]{:S(2)}) copy-start(f32[2,1,8192]{2,1,0:T(1,128)} %param.5) | copy-start | bytes 196612
  2.3 13.3 %copy-start.1 = (f32[2,1,8192]{2,1,0:T(1,128)S(1)}, f32[2,1,8192]{2,1,0:T(1,128)}, u32[]{:S(2)}) copy-start(f32[2,1,8192]{2,1,0:T(1,128)} %param.4) | copy-start | bytes 196612
  2.3 25.3 %all-to-all-start = ((bf16[16,64,128]{2,1,0:T(8,128)(2,1)}), bf16[16,64,128]{2,1,0:T(8,128)(2,1)S(1)}, u32[]{:S(2)}, u32[]{:S(2)}) async-start(bf16[16,64,128]{2,1,0:T(8,128)(2,1)} %shard_map.58), calls=%async_computation | async-start | bytes 524288 | tf_op jit(solution)/shard_map/all_to_all | solution.py:38
  15.6 10.8 %collective-permute-start = (bf16[2,64,128]{2,1,0:T(8,128)(2,1)S(1)}, bf16[2,64,128]{2,1,0:T(8,128)(2,1)S(1)}, u32[]{:S(2)}, u32[]{:S(2)}) collective-permute-start(bf16[2,64,128]{2,1,0:T(8,128)(2,1)S(1)} %reduce-precision_convert_fusion), channel_id=1, source_target_pairs={{0,0},{4,196},{64,8},{68,204},{128,16},{132,212},{192,24},{196,220... | collective-permute-start | bytes 98312 | tf_op jit(solution)/shard_map/ppermute | solution.py:152
  28.3 21.9 %all-to-all-start.1 = ((bf16[16,64,128]{2,1,0:T(8,128)(2,1)}), bf16[16,64,128]{2,1,0:T(8,128)(2,1)S(1)}, u32[]{:S(2)}, u32[]{:S(2)}) async-start(bf16[16,64,128]{2,1,0:T(8,128)(2,1)} %bitcast.6), calls=%async_computation.1 | async-start | bytes 524288 | tf_op jit(solution)/shard_map/all_to_all | solution.py:38
  38.1 6.2 %collective-permute-start.1 = (bf16[2,64,128]{2,1,0:T(8,128)(2,1)S(1)}, bf16[2,64,128]{2,1,0:T(8,128)(2,1)S(1)}, u32[]{:S(2)}, u32[]{:S(2)}) collective-permute-start(bf16[2,64,128]{2,1,0:T(8,128)(2,1)S(1)} %get-tuple-element.8), channel_id=1, source_target_pairs={{0,0},{196,4},{8,64},{204,68},{16,128},{212,132},{24,192},{220,196... | collective-permute-start | bytes 98312 | tf_op jit(solution)/shard_map/ppermute | solution.py:154

commit v8 on v7

--- a/solution.py
+++ b/solution.py
@@ -8,7 +8,7 @@
 AXES = ("rep", "fsdp")
 SHARE = 1.33 / 8
 UPPER = ((4, 7, 5, 6), (4, 5, 6, 7))
-LOWER = (((0, 3, 2, 1), (3, 1, 2, 0)), ((3, 2, 1, 0), (0, 1, 2, 3)))
+LOWER = (((0, 1, 3, 2), (3, 1, 2, 0)), ((3, 2, 1, 0), (0, 1, 2, 3)))
 
 
 def spot(rep, col, core):

time: 51.5 us -> 51.4 us (level)
  no operation moved by 1% of the time
where the time goes in v8:
time: 51.4 us; the launch traced here: 50.9 us
  starting transfers between devices  27 us (53%)
  waiting for transfers between devices  19.4 us (38%)
  Pallas kernels  3.17 us (6%)
  other arithmetic  0.69 us (1%)
  between operations  0.69 us (1%)
    all_to_all x2, starting transfers between devices, swap_rows(): lax.all_to_all(x, AXES, split_axis=0, concat_axis=0, tiled=True, axis_ind...  22.9 us
    ppermute x1, waiting for transfers between devices, body(): held = lax.ppermute(state, AXES, TO_HOLDER)  9.1 us
    all_to_all x2, waiting for transfers between devices, swap_rows(): lax.all_to_all(x, AXES, split_axis=0, concat_axis=0, tiled=True, axis_ind...  6.27 us
    ppermute x1, waiting for transfers between devices, body(): back = lax.ppermute(sums, AXES, TO_OWNER)  4 us
    ppermute x1, starting transfers between devices, body(): back = lax.ppermute(sums, AXES, TO_OWNER)  2.15 us
    ppermute x1, starting transfers between devices, body(): held = lax.ppermute(state, AXES, TO_HOLDER)  1.92 us
    pallas_call x1, Pallas kernels, listed_rows(): pl.pallas_call(listed_kernel, out_shape=jax.ShapeDtypeStruct((count,) + d...  1.66 us
  transfers between devices with their start and end apart: 4, of which 4 were waited for; matrix products, arithmetic and copies ran while one was open for 1% of the time, Pallas kernels for 0%

profile of v8, /device:TPU:25, one launch (start us, length us, event | category | flops | bytes accessed | tf_op | source)
XLA Modules:
  0.0 50.9 jit_solution(2354985612544289285)
XLA Ops:
  0.6 1.7 %shard_map.58 = bf16[16,64,128]{2,1,0:T(8,128)(2,1)} custom-call(bf16[16,8192]{1,0:T(8,128)(2,1)} %bitcast.8), custom_call_target="tpu_custom_call" | custom-call | tf_op jit(solution)/shard_map/pallas_call | solution.py:73
  2.3 0.0 copy-start
  2.3 0.0 copy-start.1
  2.3 13.3 %all-to-all-start = ((bf16[16,64,128]{2,1,0:T(8,128)(2,1)}), bf16[16,64,128]{2,1,0:T(8,128)(2,1)S(1)}, u32[]{:S(2)}, u32[]{:S(2)}) async-start(bf16[16,64,128]{2,1,0:T(8,128)(2,1)} %shard_map.58), calls=%async_computation | async-start | bytes 524288 | tf_op jit(solution)/shard_map/all_to_all | solution.py:38
  15.6 0.0 copy-done
  15.6 0.0 copy-done.1
  15.6 1.9 %collective-permute-start = (bf16[2,64,128]{2,1,0:T(8,128)(2,1)S(1)}, bf16[2,64,128]{2,1,0:T(8,128)(2,1)S(1)}, u32[]{:S(2)}, u32[]{:S(2)}) collective-permute-start(bf16[2,64,128]{2,1,0:T(8,128)(2,1)S(1)} %reduce-precision_convert_fusion), channel_id=1, source_target_pairs={{0,0},{4,196},{64,8},{68,204},{128,16},{132,212},{192,24},{196,220... | collective-permute-start | bytes 98312 | tf_op jit(solution)/shard_map/ppermute | solution.py:152
  17.6 9.1 %collective-permute-done.held_ref = bf16[2,64,128]{2,1,0:T(8,128)(2,1)S(1)} collective-permute-done((bf16[2,64,128]{2,1,0:T(8,128)(2,1)S(1)}, bf16[2,64,128]{2,1,0:T(8,128)(2,1)S(1)}, u32[]{:S(2)}, u32[]{:S(2)}) %collective-permute-start) | collective-permute-done | bytes 32800 | tf_op jit(solution)/shard_map/ppermute | solution.py:152
  26.7 1.0 %all-to-all-done = bf16[16,64,128]{2,1,0:T(8,128)(2,1)S(1)} async-done(((bf16[16,64,128]{2,1,0:T(8,128)(2,1)}), bf16[16,64,128]{2,1,0:T(8,128)(2,1)S(1)}, u32[]{:S(2)}, u32[]{:S(2)}) %all-to-all-start) | async-done | bytes 262176 | tf_op jit(solution)/shard_map/all_to_all | solution.py:38
  27.6 0.8 %shard_map.59 = (bf16[8,2,64,128]{3,2,1,0:T(8,128)(2,1)}, bf16[2,64,128]{2,1,0:T(8,128)(2,1)S(1)}) custom-call(bf16[8,2,64,128]{3,2,1,0:T(8,128)(2,1)S(1)} %bitcast.7, bf16[2,64,128]{2,1,0:T(8,128)(2,1)S(1)} %collective-permute-done.held_ref), custom_call_target="tpu_custom_call" | custom-call | tf_op jit(solution)/shard_map/pallas_call | solution.py:134
  28.4 9.7 %all-to-all-start.1 = ((bf16[16,64,128]{2,1,0:T(8,128)(2,1)}), bf16[16,64,128]{2,1,0:T(8,128)(2,1)S(1)}, u32[]{:S(2)}, u32[]{:S(2)}) async-start(bf16[16,64,128]{2,1,0:T(8,128)(2,1)} %bitcast.6), calls=%async_computation.1 | async-start | bytes 524288 | tf_op jit(solution)/shard_map/all_to_all | solution.py:38
  38.1 2.1 %collective-permute-start.1 = (bf16[2,64,128]{2,1,0:T(8,128)(2,1)S(1)}, bf16[2,64,128]{2,1,0:T(8,128)(2,1)S(1)}, u32[]{:S(2)}, u32[]{:S(2)}) collective-permute-start(bf16[2,64,128]{2,1,0:T(8,128)(2,1)S(1)} %get-tuple-element.8), channel_id=1, source_target_pairs={{0,0},{196,4},{8,64},{204,68},{16,128},{212,132},{24,192},{220,196... | collective-permute-start | bytes 98312 | tf_op jit(solution)/shard_map/ppermute | solution.py:154
  40.2 4.0 %collective-permute-done.1 = bf16[2,64,128]{2,1,0:T(8,128)(2,1)S(1)} collective-permute-done((bf16[2,64,128]{2,1,0:T(8,128)(2,1)S(1)}, bf16[2,64,128]{2,1,0:T(8,128)(2,1)S(1)}, u32[]{:S(2)}, u32[]{:S(2)}) %collective-permute-start.1) | collective-permute-done | bytes 32800 | tf_op jit(solution)/shard_map/ppermute | solution.py:154
  44.2 0.7 %multiply_add_fusion = (f32[2,64,128]{2,1,0:T(8,128)}, f32[2,64,128]{2,1,0:T(8,128)}) fusion(f32[2,64,128]{2,1,0:T(8,128)S(1)} %bitcast.10, f32[2,64,128]{2,1,0:T(8,128)S(1)} %bitcast.12, bf16[2,64,128]{2,1,0:T(8,128)(2,1)S(1)} %collective-permute-done.1), kind=kLoop, calls=%fused_computation.1 | loop fusion | flops 147456 | bytes 294912 | tf_op jit(solution)/shard_map/add | solution.py:160
  44.9 5.3 %all-to-all-done.1.listed_ref = bf16[16,64,128]{2,1,0:T(8,128)(2,1)S(1)} async-done(((bf16[16,64,128]{2,1,0:T(8,128)(2,1)}), bf16[16,64,128]{2,1,0:T(8,128)(2,1)S(1)}, u32[]{:S(2)}, u32[]{:S(2)}) %all-to-all-start.1) | async-done | bytes 262176 | tf_op jit(solution)/shard_map/all_to_all | solution.py:38
  50.2 0.8 %shard_map.60 = bf16[16,8192]{1,0:T(8,128)(2,1)} custom-call(bf16[16,64,128]{2,1,0:T(8,128)(2,1)S(1)} %all-to-all-done.1.listed_ref), custom_call_target="tpu_custom_call" | custom-call | tf_op jit(solution)/shard_map/pallas_call | solution.py:105
  (1 shorter events, 0.0 us)
Async XLA Ops:
  2.3 13.3 %copy-start = (f32[2,1,8192]{2,1,0:T(1,128)S(1)}, f32[2,1,8192]{2,1,0:T(1,128)}, u32[]{:S(2)}) copy-start(f32[2,1,8192]{2,1,0:T(1,128)} %param.5) | copy-start | bytes 196612
  2.3 13.3 %copy-start.1 = (f32[2,1,8192]{2,1,0:T(1,128)S(1)}, f32[2,1,8192]{2,1,0:T(1,128)}, u32[]{:S(2)}) copy-start(f32[2,1,8192]{2,1,0:T(1,128)} %param.4) | copy-start | bytes 196612
  2.3 25.3 %all-to-all-start = ((bf16[16,64,128]{2,1,0:T(8,128)(2,1)}), bf16[16,64,128]{2,1,0:T(8,128)(2,1)S(1)}, u32[]{:S(2)}, u32[]{:S(2)}) async-start(bf16[16,64,128]{2,1,0:T(8,128)(2,1)} %shard_map.58), calls=%async_computation | async-start | bytes 524288 | tf_op jit(solution)/shard_map/all_to_all | solution.py:38
  15.6 11.0 %collective-permute-start = (bf16[2,64,128]{2,1,0:T(8,128)(2,1)S(1)}, bf16[2,64,128]{2,1,0:T(8,128)(2,1)S(1)}, u32[]{:S(2)}, u32[]{:S(2)}) collective-permute-start(bf16[2,64,128]{2,1,0:T(8,128)(2,1)S(1)} %reduce-precision_convert_fusion), channel_id=1, source_target_pairs={{0,0},{4,196},{64,8},{68,204},{128,16},{132,212},{192,24},{196,220... | collective-permute-start | bytes 98312 | tf_op jit(solution)/shard_map/ppermute | solution.py:152
  28.4 21.8 %all-to-all-start.1 = ((bf16[16,64,128]{2,1,0:T(8,128)(2,1)}), bf16[16,64,128]{2,1,0:T(8,128)(2,1)S(1)}, u32[]{:S(2)}, u32[]{:S(2)}) async-start(bf16[16,64,128]{2,1,0:T(8,128)(2,1)} %bitcast.6), calls=%async_computation.1 | async-start | bytes 524288 | tf_op jit(solution)/shard_map/all_to_all | solution.py:38
  38.1 6.2 %collective-permute-start.1 = (bf16[2,64,128]{2,1,0:T(8,128)(2,1)S(1)}, bf16[2,64,128]{2,1,0:T(8,128)(2,1)S(1)}, u32[]{:S(2)}, u32[]{:S(2)}) collective-permute-start(bf16[2,64,128]{2,1,0:T(8,128)(2,1)S(1)} %get-tuple-element.8), channel_id=1, source_target_pairs={{0,0},{196,4},{8,64},{204,68},{16,128},{212,132},{24,192},{220,196... | collective-permute-start | bytes 98312 | tf_op jit(solution)/shard_map/ppermute | solution.py:154

commit v9 on v8

--- a/solution.py
+++ b/solution.py
@@ -115,16 +115,22 @@
     )(listed)
 
 
-def fresh_kernel(got_ref, held_ref, spread_ref, sums_ref):
+def fresh_kernel(got_ref, held_ref, spread_ref, sums_ref, fresh, sems):
     f32 = jnp.float32
+    stores = []
     for core in range(2):
         summed = got_ref[0, 1 - core].astype(f32)
         for i in range(1, 8):
             summed = summed + got_ref[i, 1 - core].astype(f32)
         sums_ref[core] = summed.astype(jnp.bfloat16)
-        fresh = (held_ref[core].astype(f32) + SHARE * summed).astype(jnp.bfloat16)
+        fresh[core] = (held_ref[core].astype(f32) + SHARE * summed).astype(jnp.bfloat16)
         for i in range(8):
-            spread_ref[i, 1 - core] = fresh
+            stores.append(
+                pltpu.make_async_copy(fresh.at[core], spread_ref.at[i, 1 - core], sems.at[core, i])
+            )
+            stores[-1].start()
+    for store in stores:
+        store.wait()
 
 
 def fresh_rows(got, held):
@@ -133,9 +139,10 @@
     held = pltpu.with_memory_space_constraint(held, pltpu.VMEM)
     return pl.pallas_call(
         fresh_kernel,
-        out_shape=[pltpu.VMEM(got.shape, got.dtype), pltpu.VMEM(held.shape, held.dtype)],
+        out_shape=[jax.ShapeDtypeStruct(got.shape, got.dtype), pltpu.VMEM(held.shape, held.dtype)],
         in_specs=[vmem] * 2,
-        out_specs=[vmem] * 2,
+        out_specs=[pl.BlockSpec(memory_space=pl.ANY), vmem],
+        scratch_shapes=[pltpu.VMEM(held.shape, held.dtype), pltpu.SemaphoreType.DMA((2, 8))],
         compiler_params=pltpu.CompilerParams(vmem_limit_bytes=4 * 2**20),
     )(got, held)
 

time: 51.4 us -> 51.5 us (level)
  no operation moved by 1% of the time
where the time goes in v9:
time: 51.5 us; the launch traced here: 51.1 us
  starting transfers between devices  27 us (52%)
  waiting for transfers between devices  19.4 us (38%)
  Pallas kernels  3.28 us (6%)
  between operations  0.7 us (1%)
  other arithmetic  0.69 us (1%)
    all_to_all x2, starting transfers between devices, swap_rows(): lax.all_to_all(x, AXES, split_axis=0, concat_axis=0, tiled=True, axis_ind...  23 us
    ppermute x1, waiting for transfers between devices, body(): held = lax.ppermute(state, AXES, TO_HOLDER)  9.1 us
    all_to_all x2, waiting for transfers between devices, swap_rows(): lax.all_to_all(x, AXES, split_axis=0, concat_axis=0, tiled=True, axis_ind...  6.27 us
    ppermute x1, waiting for transfers between devices, body(): back = lax.ppermute(sums, AXES, TO_OWNER)  4 us
    ppermute x1, starting transfers between devices, body(): back = lax.ppermute(sums, AXES, TO_OWNER)  2.15 us
    ppermute x1, starting transfers between devices, body(): held = lax.ppermute(state, AXES, TO_HOLDER)  1.92 us
    pallas_call x1, Pallas kernels, listed_rows(): pl.pallas_call(listed_kernel, out_shape=jax.ShapeDtypeStruct((count,) + d...  1.66 us
  transfers between devices with their start and end apart: 4, of which 4 were waited for; matrix products, arithmetic and copies ran while one was open for 1% of the time, Pallas kernels for 0%

profile of v9, /device:TPU:25, one launch (start us, length us, event | category | flops | bytes accessed | tf_op | source)
XLA Modules:
  0.0 51.1 jit_solution(9970623651452187256)
XLA Ops:
  0.6 1.7 %shard_map.58 = bf16[16,64,128]{2,1,0:T(8,128)(2,1)} custom-call(bf16[16,8192]{1,0:T(8,128)(2,1)} %bitcast.8), custom_call_target="tpu_custom_call" | custom-call | tf_op jit(solution)/shard_map/pallas_call | solution.py:73
  2.3 0.0 copy-start
  2.3 0.0 copy-start.1
  2.3 13.3 %all-to-all-start = ((bf16[16,64,128]{2,1,0:T(8,128)(2,1)}), bf16[16,64,128]{2,1,0:T(8,128)(2,1)S(1)}, u32[]{:S(2)}, u32[]{:S(2)}) async-start(bf16[16,64,128]{2,1,0:T(8,128)(2,1)} %shard_map.58), calls=%async_computation | async-start | bytes 524288 | tf_op jit(solution)/shard_map/all_to_all | solution.py:38
  15.6 0.0 copy-done
  15.6 0.0 copy-done.1
  15.6 1.9 %collective-permute-start = (bf16[2,64,128]{2,1,0:T(8,128)(2,1)S(1)}, bf16[2,64,128]{2,1,0:T(8,128)(2,1)S(1)}, u32[]{:S(2)}, u32[]{:S(2)}) collective-permute-start(bf16[2,64,128]{2,1,0:T(8,128)(2,1)S(1)} %reduce-precision_convert_fusion), channel_id=1, source_target_pairs={{0,0},{4,196},{64,8},{68,204},{128,16},{132,212},{192,24},{196,220... | collective-permute-start | bytes 98312 | tf_op jit(solution)/shard_map/ppermute | solution.py:159
  17.6 9.1 %collective-permute-done.held_ref = bf16[2,64,128]{2,1,0:T(8,128)(2,1)S(1)} collective-permute-done((bf16[2,64,128]{2,1,0:T(8,128)(2,1)S(1)}, bf16[2,64,128]{2,1,0:T(8,128)(2,1)S(1)}, u32[]{:S(2)}, u32[]{:S(2)}) %collective-permute-start) | collective-permute-done | bytes 32800 | tf_op jit(solution)/shard_map/ppermute | solution.py:159
  26.7 1.0 %all-to-all-done = bf16[16,64,128]{2,1,0:T(8,128)(2,1)S(1)} async-done(((bf16[16,64,128]{2,1,0:T(8,128)(2,1)}), bf16[16,64,128]{2,1,0:T(8,128)(2,1)S(1)}, u32[]{:S(2)}, u32[]{:S(2)}) %all-to-all-start) | async-done | bytes 262176 | tf_op jit(solution)/shard_map/all_to_all | solution.py:38
  27.6 0.9 %shard_map.59 = (bf16[8,2,64,128]{3,2,1,0:T(8,128)(2,1)}, bf16[2,64,128]{2,1,0:T(8,128)(2,1)S(1)}) custom-call(bf16[8,2,64,128]{3,2,1,0:T(8,128)(2,1)S(1)} %bitcast.7, bf16[2,64,128]{2,1,0:T(8,128)(2,1)S(1)} %collective-permute-done.held_ref), custom_call_target="tpu_custom_call" | custom-call | tf_op jit(solution)/shard_map/pallas_call | solution.py:140
  28.5 9.7 %all-to-all-start.1 = ((bf16[16,64,128]{2,1,0:T(8,128)(2,1)}), bf16[16,64,128]{2,1,0:T(8,128)(2,1)S(1)}, u32[]{:S(2)}, u32[]{:S(2)}) async-start(bf16[16,64,128]{2,1,0:T(8,128)(2,1)} %bitcast.6), calls=%async_computation.1 | async-start | bytes 524288 | tf_op jit(solution)/shard_map/all_to_all | solution.py:38
  38.2 2.1 %collective-permute-start.1 = (bf16[2,64,128]{2,1,0:T(8,128)(2,1)S(1)}, bf16[2,64,128]{2,1,0:T(8,128)(2,1)S(1)}, u32[]{:S(2)}, u32[]{:S(2)}) collective-permute-start(bf16[2,64,128]{2,1,0:T(8,128)(2,1)S(1)} %get-tuple-element.8), channel_id=1, source_target_pairs={{0,0},{196,4},{8,64},{204,68},{16,128},{212,132},{24,192},{220,196... | collective-permute-start | bytes 98312 | tf_op jit(solution)/shard_map/ppermute | solution.py:161
  40.3 4.0 %collective-permute-done.1 = bf16[2,64,128]{2,1,0:T(8,128)(2,1)S(1)} collective-permute-done((bf16[2,64,128]{2,1,0:T(8,128)(2,1)S(1)}, bf16[2,64,128]{2,1,0:T(8,128)(2,1)S(1)}, u32[]{:S(2)}, u32[]{:S(2)}) %collective-permute-start.1) | collective-permute-done | bytes 32800 | tf_op jit(solution)/shard_map/ppermute | solution.py:161
  44.3 0.7 %multiply_add_fusion = (f32[2,64,128]{2,1,0:T(8,128)}, f32[2,64,128]{2,1,0:T(8,128)}) fusion(f32[2,64,128]{2,1,0:T(8,128)S(1)} %bitcast.10, f32[2,64,128]{2,1,0:T(8,128)S(1)} %bitcast.12, bf16[2,64,128]{2,1,0:T(8,128)(2,1)S(1)} %collective-permute-done.1), kind=kLoop, calls=%fused_computation.1 | loop fusion | flops 147456 | bytes 294912 | tf_op jit(solution)/shard_map/add | solution.py:167
  45.0 5.3 %all-to-all-done.1.listed_ref = bf16[16,64,128]{2,1,0:T(8,128)(2,1)S(1)} async-done(((bf16[16,64,128]{2,1,0:T(8,128)(2,1)}), bf16[16,64,128]{2,1,0:T(8,128)(2,1)S(1)}, u32[]{:S(2)}, u32[]{:S(2)}) %all-to-all-start.1) | async-done | bytes 262176 | tf_op jit(solution)/shard_map/all_to_all | solution.py:38
  50.3 0.8 %shard_map.60 = bf16[16,8192]{1,0:T(8,128)(2,1)} custom-call(bf16[16,64,128]{2,1,0:T(8,128)(2,1)S(1)} %all-to-all-done.1.listed_ref), custom_call_target="tpu_custom_call" | custom-call | tf_op jit(solution)/shard_map/pallas_call | solution.py:105
  (1 shorter events, 0.0 us)
Async XLA Ops:
  2.3 13.3 %copy-start = (f32[2,1,8192]{2,1,0:T(1,128)S(1)}, f32[2,1,8192]{2,1,0:T(1,128)}, u32[]{:S(2)}) copy-start(f32[2,1,8192]{2,1,0:T(1,128)} %param.5) | copy-start | bytes 196612
  2.3 13.3 %copy-start.1 = (f32[2,1,8192]{2,1,0:T(1,128)S(1)}, f32[2,1,8192]{2,1,0:T(1,128)}, u32[]{:S(2)}) copy-start(f32[2,1,8192]{2,1,0:T(1,128)} %param.4) | copy-start | bytes 196612
  2.3 25.3 %all-to-all-start = ((bf16[16,64,128]{2,1,0:T(8,128)(2,1)}), bf16[16,64,128]{2,1,0:T(8,128)(2,1)S(1)}, u32[]{:S(2)}, u32[]{:S(2)}) async-start(bf16[16,64,128]{2,1,0:T(8,128)(2,1)} %shard_map.58), calls=%async_computation | async-start | bytes 524288 | tf_op jit(solution)/shard_map/all_to_all | solution.py:38
  15.6 11.0 %collective-permute-start = (bf16[2,64,128]{2,1,0:T(8,128)(2,1)S(1)}, bf16[2,64,128]{2,1,0:T(8,128)(2,1)S(1)}, u32[]{:S(2)}, u32[]{:S(2)}) collective-permute-start(bf16[2,64,128]{2,1,0:T(8,128)(2,1)S(1)} %reduce-precision_convert_fusion), channel_id=1, source_target_pairs={{0,0},{4,196},{64,8},{68,204},{128,16},{132,212},{192,24},{196,220... | collective-permute-start | bytes 98312 | tf_op jit(solution)/shard_map/ppermute | solution.py:159
  28.5 21.8 %all-to-all-start.1 = ((bf16[16,64,128]{2,1,0:T(8,128)(2,1)}), bf16[16,64,128]{2,1,0:T(8,128)(2,1)S(1)}, u32[]{:S(2)}, u32[]{:S(2)}) async-start(bf16[16,64,128]{2,1,0:T(8,128)(2,1)} %bitcast.6), calls=%async_computation.1 | async-start | bytes 524288 | tf_op jit(solution)/shard_map/all_to_all | solution.py:38
  38.2 6.2 %collective-permute-start.1 = (bf16[2,64,128]{2,1,0:T(8,128)(2,1)S(1)}, bf16[2,64,128]{2,1,0:T(8,128)(2,1)S(1)}, u32[]{:S(2)}, u32[]{:S(2)}) collective-permute-start(bf16[2,64,128]{2,1,0:T(8,128)(2,1)S(1)} %get-tuple-element.8), channel_id=1, source_target_pairs={{0,0},{196,4},{8,64},{204,68},{16,128},{212,132},{24,192},{220,196... | collective-permute-start | bytes 98312 | tf_op jit(solution)/shard_map/ppermute | solution.py:161
